TPU v7x, 32 devices: a whole 2x2x4 slice. The times are simulated.
32 devices in a mesh: gx: 4 (over x, core), gy: 4 (over z), gz: 2 (over y).
Axes of the slice: x: 2, y: 2, z: 4, core: 2. Of those that a mesh axis runs over, the one named last changes fastest.
Arguments:
- fine_rhs: bfloat16 [96, 96, 48, 256], P('gx', 'gy', 'gz'), may hold values from -6 to 6
- coef_table: bfloat16 [256], replicated, may hold values from 0.29882812 to 3
- coef_ids: int32 [128, 512], P(('gx', 'gy', 'gz')), may hold values from 0 to 255
- localization: int32 [128, 512], P(('gx', 'gy', 'gz')), may hold values from 0 to 32767, as said below
- patch_mask: int32 [128, 512], P(('gx', 'gy', 'gz')), may hold values from 0 to 1, as said below
- measure_weights: bfloat16 [128, 512], P(('gx', 'gy', 'gz')), may hold values from 0.5 to 2
- owners: int32 [128], P(('gx', 'gy', 'gz')), may hold values from 0 to 1, as said below
Outputs:
- coarse_stiffness: float32 [128, 4096], P(('gx', 'gy', 'gz'))
- coarse_rhs: float32 [128, 16384], P(('gx', 'gy', 'gz'))
Inputs may be any that keep to these rules, and one draw needn't show every extreme that they name: `localization`: each patch's list is a box of 8 x 8 x 8 consecutive cells of the device's block extended by 4 cells on every side (extent 24 + 2 * 4), in row-major order with the first dimension slowest; on every device the first patch's box starts at the extended block's first cell and the second's ends at its last. `patch_mask`: in every 2 x 2 x 2 subcell of a patch's box the dof whose three box coordinates are all even is live. `owners`: no device names one owner for more than 2 of its patches; in each group of devices that differ only in the gz index, one owner gets exactly 2 patches from every device of the group.
All inputs are finite; a program needn't handle non-finite values.
Results may differ from a plain program's by a relative error of at most 0.0003.
Values may be sent and summed in bfloat16 or wider, within the bound.
A program may use at most 128 MiB of HBM per device.

v0:
```python
import jax
import jax.numpy as jnp
from jax import lax
from jax.sharding import PartitionSpec as P

BOX = 8
HW = 4
PATCH = 512
M = 64


diag_shift = 6.5
highest = lax.Precision.HIGHEST


def extended_2(array, sides, width):
    for axis, dim in sides:
        size, length = (lax.axis_size(axis), array.shape[dim])
        up = [(i, (i + 1) % size) for i in range(size - 1)]
        down = [(j, i) for i, j in up]
        last = lax.slice_in_dim(array, length - width, length, axis=dim)
        first = lax.slice_in_dim(array, 0, width, axis=dim)
        before = lax.ppermute(last, axis, up)
        after = lax.ppermute(first, axis, down)
        array = jnp.concatenate([before, array, after], axis=dim)
    return array


def box_tables():
    dof_index = jnp.arange(PATCH, dtype=jnp.int32)
    along_one = dof_index // (BOX * BOX)
    along_two = dof_index // BOX % BOX
    along_three = dof_index % BOX
    distance = (
        jnp.abs(along_one[:, None] - along_one[None, :])
        + jnp.abs(along_two[:, None] - along_two[None, :])
        + jnp.abs(along_three[:, None] - along_three[None, :])
    )
    adjacency = jnp.where(distance == 1, 1.0, 0.0).astype(jnp.float32)
    half_box = BOX // 2
    subcell = (along_one // 2 * half_box + along_two // 2) * half_box + along_three // 2
    member = jnp.where(
        subcell[None, :] == jnp.arange(M, dtype=jnp.int32)[:, None], 1.0, 0.0
    ).astype(jnp.float32)
    return (adjacency, member)


def solve_patch(patch_rows, coefficient, live_mask, weights, adjacency, member):
    root_coef = jnp.sqrt(coefficient)
    coupled = (
        live_mask[:, None]
        * live_mask[None, :]
        * (diag_shift * jnp.diag(coefficient) - root_coef[:, None] * root_coef[None, :] * adjacency)
    )
    operator = coupled + jnp.diag(1.0 - live_mask)
    measure = member * (weights * live_mask)[None, :]
    factor = jnp.linalg.cholesky(operator)
    response = jax.scipy.linalg.cho_solve((factor, True), measure.T)
    schur = jnp.dot(measure, response, precision=highest)
    occupied = jnp.max(live_mask)
    identity = jnp.eye(measure.shape[0], dtype=jnp.float32)
    schur = schur + (1.0 - occupied) * identity
    small_factor = jnp.linalg.cholesky(schur)
    coarse_block = jax.scipy.linalg.cho_solve((small_factor, True), identity) * occupied
    projected = jnp.dot(response.T, patch_rows.astype(jnp.float32), precision=highest)
    coarse_part = jnp.dot(coarse_block, projected, precision=highest)
    return (coarse_block.reshape(-1), coarse_part.reshape(-1))


def local(fine_rhs, coef_table, coef_ids, localization, patch_mask, measure_weights, owners):
    adjacency, member = box_tables()
    extended = extended_2(fine_rhs, (("gx", 0), ("gy", 1), ("gz", 2)), HW)
    flattened = extended.reshape(-1, extended.shape[-1])
    patch_rows = jnp.take(flattened, localization, axis=0)
    table_hits = (
        coef_ids[:, :, None] == jnp.arange(coef_table.shape[0], dtype=jnp.int32)[None, None, :]
    )
    coefficient = jnp.sum(
        jnp.where(table_hits, coef_table.astype(jnp.float32)[None, None, :], 0.0), axis=-1
    )
    live_mask = patch_mask.astype(jnp.float32)
    weights = measure_weights.astype(jnp.float32)
    patch_count = localization.shape[0]
    groups = lax.axis_size("gz")
    capacity = max(patch_count // 4, (patch_count + groups - 1) // groups)
    slot_count = groups * capacity
    owner_hits = (owners[:, None] == jnp.arange(groups, dtype=jnp.int32)[None, :]).astype(jnp.int32)
    earlier_hits = jnp.cumsum(owner_hits, axis=0) - owner_hits
    slot_rank = jnp.sum(earlier_hits * owner_hits, axis=1)
    target_slot = owners * capacity + slot_rank
    placing = jnp.where(
        jnp.arange(slot_count, dtype=jnp.int32)[:, None] == target_slot[None, :], 1.0, 0.0
    )
    placing = placing.astype(jnp.float32)
    extras = jnp.stack([coefficient, live_mask, weights], axis=1).astype(jnp.bfloat16)
    place_half = placing.astype(jnp.bfloat16)
    sent_rows = jnp.einsum(
        "sp,pjf->sjf", place_half, patch_rows, preferred_element_type=jnp.float32
    )
    sent_rows = sent_rows.astype(jnp.bfloat16).reshape((groups, capacity) + patch_rows.shape[1:])
    sent_extras = jnp.einsum("sp,pjf->sjf", place_half, extras, preferred_element_type=jnp.float32)
    sent_extras = sent_extras.astype(jnp.bfloat16).reshape((groups, capacity) + extras.shape[1:])
    item_rows = lax.all_to_all(sent_rows, "gz", split_axis=0, concat_axis=0, tiled=True)
    item_extras = lax.all_to_all(sent_extras, "gz", split_axis=0, concat_axis=0, tiled=True)
    leading = item_rows.shape[:2]
    rows_all = item_rows.reshape((-1,) + item_rows.shape[2:])
    wide = item_extras.reshape((-1,) + item_extras.shape[2:]).astype(jnp.float32)
    blocks, rhs_parts = jax.vmap(solve_patch, in_axes=(0, 0, 0, 0, None, None))(
        rows_all, wide[:, 0], wide[:, 1], wide[:, 2], adjacency, member
    )
    received_blocks = blocks.reshape(leading + (-1,))
    received_rhs = rhs_parts.reshape(leading + (-1,))
    coarse_stiffness = received_blocks.reshape(slot_count, -1)
    coarse_rhs = received_rhs.reshape(slot_count, -1)
    return (coarse_stiffness, coarse_rhs)


def solution(mesh):
    placed = (
        P("gx", "gy", "gz", None),
        P(),
        P(("gx", "gy", "gz"), None),
        P(("gx", "gy", "gz"), None),
        P(("gx", "gy", "gz"), None),
        P(("gx", "gy", "gz"), None),
        P(("gx", "gy", "gz")),
    )
    return jax.shard_map(
        local,
        mesh=mesh,
        in_specs=placed,
        out_specs=(P(("gx", "gy", "gz"), None), P(("gx", "gy", "gz"), None)),
        check_vma=False,
    )
```

profile of v0, /device:TPU:1, one launch (start us, length us, event | category | flops | bytes accessed | tf_op | source)
XLA Modules:
  0.0 722.7 jit_solution(13713088251644839654)
XLA Ops:
  7.1 3.8 all-to-all-start
  10.9 3.3 fusion.113
  14.2 4.5 collective-permute-start
  35.3 4.2 fusion.2
  41.5 46.9 %custom-call.49 = f32[4,128,128]{2,1,0:T(8,128)S(1)} custom-call(f32[4,128,128]{2,1,0:T(8,128)S(1)} %cholesky.314), custom_call_target="Cholesky" | custom-call | tf_op jit(solution)/shard_map/vmap(jit(cholesky))/cholesky | solution.py:57
  88.4 39.3 %custom-call.50 = f32[4,1,128,128]{2,3,1,0:T(8,128)S(1)} custom-call(f32[4,1,128,128]{3,2,1,0:T(8,128)S(1)} %select_bitcast_fusion.2), custom_call_target="InvertDiagBlocksLowerTriangular" | custom-call | tf_op jit(solution)/shard_map/vmap(jit(cholesky))/cholesky | solution.py:57
  135.2 47.1 %custom-call.51 = f32[4,128,128]{2,1,0:T(8,128)S(1)} custom-call(f32[4,128,128]{2,1,0:T(8,128)S(1)} %cholesky.318), custom_call_target="Cholesky" | custom-call | tf_op jit(solution)/shard_map/vmap(jit(cholesky))/cholesky | solution.py:57
  183.1 39.3 %custom-call.52 = f32[4,1,128,128]{2,3,1,0:T(8,128)S(1)} custom-call(f32[4,1,128,128]{3,2,1,0:T(8,128)S(1)} %get-tuple-element.33), custom_call_target="InvertDiagBlocksLowerTriangular" | custom-call | tf_op jit(solution)/shard_map/vmap(jit(cholesky))/cholesky | solution.py:57
  226.6 46.9 %custom-call.53 = f32[4,128,128]{2,1,0:T(8,128)S(1)} custom-call(f32[4,128,128]{2,1,0:T(8,128)S(1)} %cholesky.323), custom_call_target="Cholesky" | custom-call | tf_op jit(solution)/shard_map/vmap(jit(cholesky))/cholesky | solution.py:57
  274.3 39.7 %custom-call.54 = f32[4,1,128,128]{2,3,1,0:T(8,128)S(1)} custom-call(f32[4,1,128,128]{3,2,1,0:T(8,128)S(1)} %get-tuple-element.31), custom_call_target="InvertDiagBlocksLowerTriangular" | custom-call | tf_op jit(solution)/shard_map/vmap(jit(cholesky))/cholesky | solution.py:57
  317.7 46.9 %custom-call.55 = f32[4,128,128]{2,1,0:T(8,128)S(1)} custom-call(f32[4,128,128]{2,1,0:T(8,128)S(1)} %convolution_subtract_fusion.2), custom_call_target="Cholesky" | custom-call | tf_op jit(solution)/shard_map/vmap(jit(cholesky))/cholesky | solution.py:57
  365.9 5.0 select_select_fusion
  370.9 14.8 %while.1 = (s32[]{:T(128)}, f32[4,512,512]{2,1,0:T(8,128)}, s32[4,2]{0,1:T(2,128)S(1)}, f32[4,4,128,128]{3,2,0,1:T(8,128)}, s32[]{:T(128)}) while((s32[]{:T(128)}, f32[4,512,512]{2,1,0:T(8,128)}, s32[4,2]{0,1:T(2,128)S(1)}, f32[4,4,128,128]{3,2,0,1:T(8,128)}, s32[]{:T(128)}) %tuple.43), condition=%wide.while_cond, body=%wide.while_body.sunk | while | flops 2 | bytes 525921 | solution.py:58
  371.5 3.1 bitcast_dynamic-update-slice_fusion.2
  375.3 3.1 bitcast_dynamic-update-slice_fusion.2
  379.0 3.1 bitcast_dynamic-update-slice_fusion.2
  385.8 158.2 %custom-call.56 = f32[4,4,128,128]{2,3,1,0:T(8,128)S(1)} custom-call(f32[4,4,128,128]{3,2,1,0:T(8,128)} %bitcast.122), custom_call_target="InvertDiagBlocksLowerTriangular" | custom-call | tf_op jit(solution)/shard_map/vmap(jit(_cho_solve))/triangular_solve | solution.py:58
  547.4 3.5 constant_dynamic-update-slice_fusion.1
  551.3 3.7 collective-permute-start.2
  560.5 28.2 %collective-permute-done.2 = bf16[32,4,24,256]{3,2,1,0:T(8,128)(2,1)S(1)} collective-permute-done((bf16[32,4,24,256]{3,2,1,0:T(8,128)(2,1)S(1)}, bf16[32,4,24,256]{3,2,1,0:T(8,128)(2,1)S(1)}, u32[]{:S(2)}, u32[]{:S(2)}) %collective-permute-start.2) | collective-permute-done | bytes 1572896 | tf_op jit(solution)/shard_map/ppermute | solution.py:23
  588.7 4.2 collective-permute-done.3
  597.2 5.0 collective-permute-start.4
  614.3 25.0 %custom-call.57 = f32[4,64,64]{2,1,0:T(8,128)} custom-call(f32[4,64,64]{2,1,0:T(8,128)} %fusion.59), custom_call_target="Cholesky" | custom-call | tf_op jit(solution)/shard_map/vmap(jit(cholesky))/cholesky | solution.py:63
  640.3 5.6 collective-permute-done.4
  646.0 3.6 copy.125
  649.5 3.4 collective-permute-done.5
  652.9 3.6 copy.126
  656.5 16.7 %pad_maximum_fusion = bf16[32,32,32,256]{3,2,1,0:T(8,128)(2,1)} fusion(bf16[32,32,4,256]{3,2,1,0:T(4,128)(2,1)S(1)} %copy.126, bf16[32,4,24,256]{3,2,1,0:T(8,128)(2,1)S(1)} %collective-permute-done.3, bf16[32,24,24,256]{3,2,1,0:T(8,128)(2,1)} %copy-done, bf16[32,4,24,256]{3,2,1,0:T(8,128)(2,1)S(1)} %collective-permute-done.2, ...), kind=kLoop, calls=%fused_computation.3 | loop fusion | flops 83886080 | bytes 33554432 | tf_op jit(solution)/shard_map/concatenate | solution.py:25
  673.2 14.6 %gather_fusion = bf16[2048,256]{1,0:T(8,128)(2,1)S(1)} fusion(bf16[32768,256]{1,0:T(8,128)(2,1)} %bitcast.116, s32[2048]{0:T(1024)S(1)} %copy-done.19), kind=kCustom, calls=%fused_computation | custom fusion | bytes 2105344 | tf_op jit(solution)/shard_map/jit(_take)/gather | solution.py:74
  687.8 5.0 convolution_convert_fusion
  695.4 3.6 all-to-all-start.1
  699.1 19.7 %custom-call.58 = f32[4,1,64,64]{2,3,1,0:T(8,128)S(1)} custom-call(f32[4,1,64,64]{3,2,1,0:T(8,128)S(1)} %select_bitcast_fusion.3), custom_call_target="InvertDiagBlocksLowerTriangular" | custom-call | tf_op jit(solution)/shard_map/vmap(jit(_cho_solve))/triangular_solve | solution.py:64
  (154 shorter events, 81.2 us)
Async XLA Ops:
  0.6 21.7 %copy-start.17 = (s32[4,512]{1,0:T(4,128)S(1)}, s32[4,512]{1,0:T(4,128)}, u32[]{:S(2)}) copy-start(s32[4,512]{1,0:T(4,128)} %param.10) | copy-start | bytes 24580
  2.8 2.8 copy-start.21
  7.1 22.8 %all-to-all-start = ((bf16[2,2,3,512]{3,1,2,0:T(2,128)(2,1)}), bf16[2,2,3,512]{3,1,2,0:T(2,128)(2,1)}, u32[]{:S(2)}, u32[]{:S(2)}) async-start(bf16[2,2,3,512]{3,1,2,0:T(2,128)(2,1)} %copy.103), calls=%async_computation | async-start | bytes 24576 | tf_op jit(solution)/shard_map/all_to_all | solution.py:104
  14.2 531.8 %collective-permute-start = (bf16[4,24,24,256]{3,2,1,0:T(8,128)(2,1)}, bf16[4,24,24,256]{3,2,1,0:T(8,128)(2,1)}, u32[]{:S(2)}, u32[]{:S(2)}) collective-permute-start(bf16[4,24,24,256]{3,2,1,0:T(8,128)(2,1)} %get-tuple-element.29), channel_id=1, source_target_pairs={{0,8},{8,16},{16,24},{1,9},{9,17},{17,25},{2,10},{10,18},{18,26},{... | collective-permute-start | bytes 3538952 | tf_op jit(solution)/shard_map/ppermute | solution.py:23
  18.7 532.2 %collective-permute-start.1 = (bf16[4,24,24,256]{3,2,1,0:T(8,128)(2,1)}, bf16[4,24,24,256]{3,2,1,0:T(8,128)(2,1)S(1)}, u32[]{:S(2)}, u32[]{:S(2)}) collective-permute-start(bf16[4,24,24,256]{3,2,1,0:T(8,128)(2,1)} %get-tuple-element.28), channel_id=1, source_target_pairs={{8,0},{16,8},{24,16},{9,1},{17,9},{25,17},{10,2},{18,10},{26,18},{... | collective-permute-start | bytes 3538952 | tf_op jit(solution)/shard_map/ppermute | solution.py:24
  39.5 1.9 copy-start.2
  135.2 229.4 %copy-start.14 = (pred[128,128]{1,0:T(8,128)(4,1)S(1)}, pred[128,128]{1,0:T(8,128)(4,1)}, u32[]{:S(2)}) copy-start(pred[128,128]{1,0:T(8,128)(4,1)} %iota_compare_fusion.7) | copy-start | bytes 49156
  365.9 5.0 copy-start.23
  365.9 19.8 %copy-start.10 = (f32[512,64]{0,1:T(8,128)S(1)}, f32[512,64]{0,1:T(8,128)}, u32[]{:S(2)}) copy-start(f32[512,64]{0,1:T(8,128)} %fusion.61) | copy-start | bytes 393220
  365.9 19.8 %copy-start.18 = (f32[4,512]{1,0:T(4,128)S(1)}, f32[4,512]{1,0:T(4,128)}, u32[]{:S(2)}) copy-start(f32[4,512]{1,0:T(4,128)} %get-tuple-element.39) | copy-start | bytes 24580
  385.8 165.1 %copy-start.5 = (f32[4,512,64]{1,2,0:T(8,128)}, f32[4,512,64]{1,2,0:T(8,128)S(1)}, u32[]{:S(2)}) copy-start(f32[4,512,64]{1,2,0:T(8,128)S(1)} %broadcast_multiply_fusion) | copy-start | bytes 1572868
  544.1 6.8 copy-start.3
  550.9 6.0 copy-start.1
  550.9 5.6 copy-start.4
  550.9 6.0 copy-start.6
  551.0 41.8 %copy-start = (bf16[32,24,24,256]{3,2,1,0:T(8,128)(2,1)}, bf16[32,24,24,256]{3,2,1,0:T(8,128)(2,1)S(1)}, u32[]{:S(2)}) copy-start(bf16[32,24,24,256]{3,2,1,0:T(8,128)(2,1)S(1)} %constant_dynamic-update-slice_fusion) | copy-start | bytes 28311556
  551.3 37.4 %collective-permute-start.2 = (bf16[32,4,24,256]{3,2,1,0:T(8,128)(2,1)S(1)}, bf16[32,4,24,256]{3,2,1,0:T(8,128)(2,1)S(1)}, u32[]{:S(2)}, u32[]{:S(2)}) collective-permute-start(bf16[32,4,24,256]{3,2,1,0:T(8,128)(2,1)S(1)} %get-tuple-element.26), channel_id=1, source_target_pairs={{0,2},{2,4},{4,6},{1,3},{3,5},{5,7},{8,10},{10,12},{12,14},{9,11},... | collective-permute-start | bytes 4718600 | tf_op jit(solution)/shard_map/ppermute | solution.py:23
  555.0 37.9 %collective-permute-start.3 = (bf16[32,4,24,256]{3,2,1,0:T(8,128)(2,1)S(1)}, bf16[32,4,24,256]{3,2,1,0:T(8,128)(2,1)S(1)}, u32[]{:S(2)}, u32[]{:S(2)}) collective-permute-start(bf16[32,4,24,256]{3,2,1,0:T(8,128)(2,1)S(1)} %get-tuple-element.27), channel_id=1, source_target_pairs={{2,0},{4,2},{6,4},{3,1},{5,3},{7,5},{10,8},{12,10},{14,12},{11,9},... | collective-permute-start | bytes 4718600 | tf_op jit(solution)/shard_map/ppermute | solution.py:24
  597.2 11.7 %copy-start.12 = (f32[64,512]{1,0:T(8,128)S(1)}, f32[64,512]{1,0:T(8,128)}, u32[]{:S(2)}) copy-start(f32[64,512]{1,0:T(8,128)} %fusion.60) | copy-start | bytes 393220
  597.2 48.7 %collective-permute-start.4 = (bf16[32,32,4,256]{3,1,2,0:T(8,128)(2,1)}, bf16[32,32,4,256]{3,1,2,0:T(8,128)(2,1)}, u32[]{:S(2)}, u32[]{:S(2)}) collective-permute-start(bf16[32,32,4,256]{3,1,2,0:T(8,128)(2,1)} %copy.123), channel_id=1, source_target_pairs={{0,1},{2,3},{4,5},{6,7},{8,9},{10,11},{12,13},{14,15},{16,17},{18,... | collective-permute-start | bytes 6291464 | tf_op jit(solution)/shard_map/ppermute | solution.py:23
  602.2 37.1 %copy-start.16 = (pred[64,64]{1,0:T(8,128)(4,1)S(1)}, pred[64,64]{1,0:T(8,128)(4,1)}, u32[]{:S(2)}) copy-start(pred[64,64]{1,0:T(8,128)(4,1)} %iota_compare_fusion.9) | copy-start | bytes 12292
  604.0 48.9 %collective-permute-start.5 = (bf16[32,32,4,256]{3,1,2,0:T(8,128)(2,1)}, bf16[32,32,4,256]{3,1,2,0:T(8,128)(2,1)}, u32[]{:S(2)}, u32[]{:S(2)}) collective-permute-start(bf16[32,32,4,256]{3,1,2,0:T(8,128)(2,1)} %copy.124), channel_id=1, source_target_pairs={{1,0},{3,2},{5,4},{7,6},{9,8},{11,10},{13,12},{15,14},{17,16},{19,... | collective-permute-start | bytes 6291464 | tf_op jit(solution)/shard_map/ppermute | solution.py:24
  608.3 0.7 copy-start.7
  656.5 16.7 %copy-start.19 = (s32[2048]{0:T(1024)S(1)}, s32[2048]{0:T(1024)}, u32[]{:S(2)}) copy-start(s32[2048]{0:T(1024)} %broadcast_clamp_fusion) | copy-start | bytes 24580
  673.2 14.6 %copy-start.13 = (pred[4,512]{0,1:T(8,128)(4,1)S(1)}, pred[4,512]{0,1:T(8,128)(4,1)}, u32[]{:S(2)}) copy-start(pred[4,512]{0,1:T(8,128)(4,1)} %copy.122) | copy-start | bytes 6148
  673.2 14.6 %copy-start.22 = (s32[4]{0:T(128)S(1)}, s32[4]{0:T(128)}, u32[]{:S(2)}) copy-start(s32[4]{0:T(128)} %copy-done.21) | copy-start | bytes 52
  692.9 6.1 copy-start.9
  692.9 6.1 copy-start.15
  692.9 25.9 %copy-start.11 = (f32[64,64]{1,0:T(8,128)S(1)}, f32[64,64]{1,0:T(8,128)}, u32[]{:S(2)}) copy-start(f32[64,64]{1,0:T(8,128)} %get-tuple-element.53) | copy-start | bytes 49156
  692.9 26.3 %copy-start.20 = (f32[4]{0:T(128)S(1)}, f32[4]{0:T(128)}, u32[]{:S(2)}) copy-start(f32[4]{0:T(128)} %get-tuple-element.35) | copy-start | bytes 52
  693.7 26.6 %copy-start.8 = (f32[4,128,64]{1,2,0:T(8,128)S(1)}, f32[4,128,64]{1,2,0:T(8,128)}, u32[]{:S(2)}) copy-start(f32[4,128,64]{1,2,0:T(8,128)} %copy-done.7) | copy-start | bytes 393220
  695.4 24.8 %all-to-all-start.1 = ((bf16[2,2,512,256]{3,1,2,0:T(2,128)(2,1)}), bf16[2,2,512,256]{3,1,2,0:T(2,128)(2,1)S(1)}, u32[]{:S(2)}, u32[]{:S(2)}) async-start(bf16[2,2,512,256]{3,1,2,0:T(2,128)(2,1)} %copy.128), calls=%async_computation.1 | async-start | bytes 2097152 | tf_op jit(solution)/shard_map/all_to_all | solution.py:103
where the time goes:
time: 735 us; the launch traced here: 723 us
  other arithmetic  559 us (76%)
  local copies, waits for them, and re-layouts  64.5 us (9%)
  waiting for transfers between devices  41.4 us (6%)
  matrix products  30.3 us (4%)
  starting transfers between devices  25.3 us (3%)
    another operation x18, other arithmetic, solve_patch(): factor = jnp.linalg.cholesky(operator)  310 us
    another operation x4, other arithmetic, solve_patch(): response = jax.scipy.linalg.cho_solve((factor, True), measure.T)  164 us
    ppermute x3, waiting for transfers between devices, extended_2(): before = lax.ppermute(last, axis, up)  33.8 us
    another operation x4, other arithmetic, solve_patch(): small_factor = jnp.linalg.cholesky(schur)  26.7 us
    another operation x3, other arithmetic, solve_patch(): jax.scipy.linalg.cho_solve((small_factor, True), identity) * occupied  20.4 us
    concatenate x1, other arithmetic, extended_2(): array = jnp.concatenate([before, array, after], axis=dim)  16.7 us
    another operation x12, local copies, waits for them, and re-layouts  14.8 us
  transfers between devices with their start and end apart: 8, of which 4 were waited for; matrix products, arithmetic and copies ran while one was open for 82% of the time, Pallas kernels for 0%

commit v1 on v0

v1 whole, which is shorter than its diff:
```python
import math
import jax
import jax.numpy as jnp
from jax import lax
from jax.experimental import pallas as pl
from jax.experimental.pallas import tpu as pltpu
from jax.sharding import PartitionSpec as P

BOX = 8
HW = 4
PATCH = 512
M = 64
HALF = BOX // 2

diag_shift = 6.5
radius = 6.0 * math.cos(math.pi / 9.0) / diag_shift
low, high = (1.0 - radius) * diag_shift, (1.0 + radius) * diag_shift
half_steps = 30
newton_steps = 4
highest = lax.Precision.HIGHEST


def relaxation():
    weights = [1.0, 2.0 / (2.0 - radius * radius)]
    while len(weights) < half_steps:
        weights.append(1.0 / (1.0 - radius * radius * weights[-1] / 4.0))
    return weights


def start_polynomial():
    a, b = 1.0 / high, 1.0 / low
    mid, half = (a + b) / 2.0, (b - a) / 2.0
    t = -mid / half
    top = 4.0 * t**3 - 3.0 * t
    c3 = 4.0 / half**3 / top
    c2 = -12.0 * mid / half**3 / top
    c1 = (12.0 * mid * mid / half**3 - 3.0 / half) / top
    return (-c1, -c2, -c3)


def exact_dot(a, b):
    return jnp.dot(a, b, precision=highest, preferred_element_type=jnp.float32)


def relax(new, old, bias, gate, weight, flip, place):
    for x in range(BOX):
        here = old[x]
        up = pltpu.roll(here, 1, 1)
        down = pltpu.roll(here, BOX - 1, 1)
        total = jnp.where(place == 0, 0.0, up) + jnp.where(place == BOX - 1, 0.0, down)
        zero = jnp.zeros_like(here[:1])
        before = jnp.concatenate([zero, here[:-1]], axis=0)
        after = jnp.concatenate([here[1:], zero], axis=0)
        odd = (place + (x + flip)) % 2
        total = total + here + jnp.where(odd == 0, before, after)
        if x > 0:
            total = total + old[x - 1]
        if x < BOX - 1:
            total = total + old[x + 1]
        current = new[x]
        new[x] = current + weight * (gate[x] * total + bias[x] - current)


def patch_kernel(slot_ref, omega_ref, dofs_ref, rows_ref, block_ref, part_ref,
                 red, black, bias_r, bias_k, gate_r, gate_k, root_r, root_k):
    patches = rows_ref.shape[0]
    lanes = patches * M
    spot = jnp.where(
        lax.broadcasted_iota(jnp.int32, (patches, lanes), 1) // M
        == lax.broadcasted_iota(jnp.int32, (patches, lanes), 0), 1.0, 0.0).astype(jnp.bfloat16)
    shape = (HALF, BOX, lanes)
    place = lax.broadcasted_iota(jnp.int32, shape, 1)
    column = lax.broadcasted_iota(jnp.int32, shape, 2) % M
    along = lax.broadcasted_iota(jnp.int32, shape, 0)
    for color, (bias, gate, root) in enumerate(((bias_r, gate_r, root_r), (bias_k, gate_k, root_k))):
        wide = [
            jnp.dot(dofs_ref[color, kind], spot, preferred_element_type=jnp.float32).reshape(
                (BOX, HALF, BOX, lanes))
            for kind in range(3)
        ]
        for x in range(BOX):
            live = wide[1][x]
            scale = live * lax.rsqrt(wide[0][x])
            member = (x // 2 * HALF + along) * HALF + place // 2 == column
            root[x] = scale
            gate[x] = live * (1.0 / diag_shift)
            bias[x] = jnp.where(member, scale * wide[2][x] * (1.0 / diag_shift), 0.0)
    red[...] = bias_r[...]
    black[...] = jnp.zeros(black.shape, jnp.float32)
    relax(black, red, bias_k, gate_k, omega_ref[1], 1, place)

    @pl.loop(1, half_steps // 2)
    def _(step):
        relax(red, black, bias_r, gate_r, omega_ref[2 * step], 0, place)
        relax(black, red, bias_k, gate_k, omega_ref[2 * step + 1], 1, place)

    pooled, norms, response = [], [], []
    for x2 in range(BOX // 2):
        solved, size = 0.0, 0.0
        for x in (2 * x2, 2 * x2 + 1):
            for color, (grid, bias, root) in enumerate(((red, bias_r, root_r), (black, bias_k, root_k))):
                solved = solved + reduce_weight(dofs_ref, spot, color, x, lanes) * root[x] * grid[x]
                size = size + bias[x] * bias[x]
            first = red[x] * root_r[x]
            second = black[x] * root_k[x]
            odd = (place + x) % 2
            response.append(jnp.stack(
                [jnp.where(odd == 0, first, second), jnp.where(odd == 0, second, first)], axis=1))
        pooled.append(solved)
        norms.append(size)
    pooled = jnp.stack(pooled).reshape((2 * M, lanes))
    norms = jnp.stack(norms).reshape((2 * M, lanes)) * (diag_shift * diag_shift)
    pairs = jnp.where(
        lax.broadcasted_iota(jnp.int32, (M, 2 * M), 1) // 2
        == lax.broadcasted_iota(jnp.int32, (M, 2 * M), 0), 1.0, 0.0)
    schur = exact_dot(pairs, pooled)
    norms = exact_dot(pairs, norms)
    response = jnp.stack(response).reshape((PATCH, lanes))
    coarse = response.astype(jnp.bfloat16)
    fine = (response - coarse.astype(jnp.float32)).astype(jnp.bfloat16)
    coarse, fine = coarse.T, fine.T
    if part_ref.shape[0] > patches:
        block_ref[...] = jnp.zeros(block_ref.shape, jnp.float32)
        part_ref[...] = jnp.zeros(part_ref.shape, jnp.float32)
    identity = jnp.where(
        lax.broadcasted_iota(jnp.int32, (M, M), 0) == lax.broadcasted_iota(jnp.int32, (M, M), 1), 1.0, 0.0)
    p0, p1, p2 = start_polynomial()
    scaled, scales, inverse = [], [], []
    for p in range(patches):
        mine = slice(p * M, (p + 1) * M)
        size = norms[:, mine]
        down = lax.rsqrt(jnp.sum(size, axis=1, keepdims=True))
        across = lax.rsqrt(jnp.sum(size, axis=0, keepdims=True))
        scales.append((down, across))
        scaled.append(schur[:, mine] * down * across)
    for s in scaled:
        inverse.append(p0 * identity + p1 * s + p2 * exact_dot(s, s))
    for _ in range(newton_steps):
        rest = [2.0 * identity - exact_dot(s, g) for s, g in zip(scaled, inverse)]
        inverse = [exact_dot(g, r) for g, r in zip(inverse, rest)]
    for p in range(patches):
        mine = slice(p * M, (p + 1) * M)
        rows = rows_ref[p]
        projected = (jnp.dot(coarse[mine], rows, preferred_element_type=jnp.float32)
                     + jnp.dot(fine[mine], rows, preferred_element_type=jnp.float32))
        down, across = scales[p]
        block = inverse[p] * down * across
        block_ref[slot_ref[p]] = block
        part_ref[slot_ref[p]] = exact_dot(block, projected)


def reduce_weight(dofs_ref, spot, color, x, lanes):
    block = dofs_ref[color, 2, x * HALF * BOX:(x + 1) * HALF * BOX]
    return jnp.dot(block, spot, preferred_element_type=jnp.float32).reshape((HALF, BOX, lanes))


def two_colors(values):
    patches = values.shape[0]
    cells = values.reshape(patches, BOX, HALF, 2, BOX)
    odd = (jnp.arange(BOX)[:, None, None] + jnp.arange(BOX)[None, None, :]) % 2
    first, second = cells[:, :, :, 0], cells[:, :, :, 1]
    both = jnp.stack([jnp.where(odd == 0, first, second), jnp.where(odd == 0, second, first)])
    return both.reshape(2, patches, PATCH // 2).transpose(0, 2, 1)


def coarse_parts(target_slot, slot_count, coefficient, live, weights, patch_rows):
    dofs = jnp.stack([two_colors(v.astype(jnp.bfloat16)) for v in (coefficient, live, weights)], axis=1)
    patches = patch_rows.shape[0]
    lanes = patches * M
    omega = jnp.array(relaxation(), jnp.float32)
    smem = pl.BlockSpec(memory_space=pltpu.SMEM)
    vmem = pl.BlockSpec(memory_space=pltpu.VMEM)
    grid = pltpu.VMEM((BOX, HALF, BOX, lanes), jnp.float32)
    return pl.pallas_call(
        patch_kernel,
        out_shape=(jax.ShapeDtypeStruct((slot_count, M, M), jnp.float32),
                   jax.ShapeDtypeStruct((slot_count, M, patch_rows.shape[-1]), jnp.float32)),
        in_specs=[smem, smem, vmem, vmem],
        out_specs=(vmem, vmem),
        scratch_shapes=[grid] * 8,
        compiler_params=pltpu.CompilerParams(vmem_limit_bytes=40 * 1024 * 1024),
        cost_estimate=pl.CostEstimate(flops=10**9, bytes_accessed=2**21, transcendentals=0),
        name="patches",
    )(target_slot, omega, dofs, patch_rows)


def extended_2(array, sides, width):
    for axis, dim in sides:
        size, length = (lax.axis_size(axis), array.shape[dim])
        up = [(i, (i + 1) % size) for i in range(size - 1)]
        down = [(j, i) for i, j in up]
        last = lax.slice_in_dim(array, length - width, length, axis=dim)
        first = lax.slice_in_dim(array, 0, width, axis=dim)
        before = lax.ppermute(last, axis, up)
        after = lax.ppermute(first, axis, down)
        array = jnp.concatenate([before, array, after], axis=dim)
    return array


def local(fine_rhs, coef_table, coef_ids, localization, patch_mask, measure_weights, owners):
    extended = extended_2(fine_rhs, (("gx", 0), ("gy", 1), ("gz", 2)), HW)
    patch_count = localization.shape[0]
    extent = extended.shape[:3]
    rows = []
    for p in range(patch_count):
        first = localization[p, 0]
        corner = (first // (extent[1] * extent[2]), first // extent[2] % extent[1], first % extent[2], 0)
        box = lax.dynamic_slice(extended, corner, (BOX, BOX, BOX, extended.shape[-1]))
        rows.append(box.reshape(PATCH, -1))
    patch_rows = jnp.stack(rows)
    table_hits = (
        coef_ids[:, :, None] == jnp.arange(coef_table.shape[0], dtype=jnp.int32)[None, None, :]
    )
    coefficient = jnp.sum(
        jnp.where(table_hits, coef_table.astype(jnp.float32)[None, None, :], 0.0), axis=-1
    )
    groups = lax.axis_size("gz")
    capacity = max(patch_count // 4, (patch_count + groups - 1) // groups)
    slot_count = groups * capacity
    same = owners[:, None] == owners[None, :]
    earlier = jnp.arange(patch_count)[:, None] > jnp.arange(patch_count)[None, :]
    slot_rank = jnp.sum(jnp.where(same & earlier, 1, 0), axis=1).astype(jnp.int32)
    target_slot = owners * capacity + slot_rank
    blocks, parts = coarse_parts(target_slot, slot_count, coefficient, patch_mask, measure_weights, patch_rows)
    blocks = lax.all_to_all(blocks, "gz", split_axis=0, concat_axis=0, tiled=True)
    parts = lax.all_to_all(parts, "gz", split_axis=0, concat_axis=0, tiled=True)
    return (blocks.reshape(slot_count, -1), parts.reshape(slot_count, -1))


def solution(mesh):
    axes = ("gx", "gy", "gz")
    each = P(axes, None)
    return jax.shard_map(
        local,
        mesh=mesh,
        in_specs=(P("gx", "gy", "gz", None), P(), each, each, each, each, P(axes)),
        out_specs=(each, each),
        check_vma=False,
    )
```

time: 735 us -> 145 us (0.20); the launches traced: 723 us -> 144 us
  other arithmetic: 559 us -> 18.4 us
  local copies, waits for them, and re-layouts: 64.5 us -> 23.5 us
  matrix products: 30.3 us -> 0 us
  waiting for transfers between devices: 41.4 us -> 55.8 us
  between operations: 1.76 us -> 11.5 us
  Pallas kernels: 0 us -> 9.07 us
    another operation x31 -> x4, other arithmetic: 521 us -> 0.24 us  [the longest x1 0.13 us: local(): patch_rows = jnp.stack(rows)]
    another operation x22 -> x0, matrix products: 22.1 us -> none  [the longest x6 12.8 us: solve_patch(): factor = jnp.linalg.cholesky(operator)]
    another operation x17 -> x3, local copies, waits for them, and re-layouts: 17.4 us -> 0.55 us  [two_colors(): jnp.stack([jnp.where(odd == 0, first, second), jnp.where(odd == 0, second...]
    gather x1 -> x0, local copies, waits for them, and re-layouts: 14.6 us -> none  [local(): patch_rows = jnp.take(flattened, localization, axis=0)]
    ppermute x3, waiting for transfers between devices: 33.8 us -> 45.1 us  [extended_2(): before = lax.ppermute(last, axis, up)]
    pallas_call x0 -> x1, Pallas kernels: none -> 9.07 us  [coarse_parts(): pl.pallas_call(patch_kernel, out_shape=(jax.ShapeDtypeStruct((slot_count,...]
    dot_general x5 -> x0, matrix products: 8.18 us -> none  [the longest x1 5.04 us: local(): jnp.einsum('sp,pjf->sjf', place_half, patch_rows, preferred_element_type=...]
  transfers between devices with their start and end apart: 8 -> 7, of which waited for: 4 -> 7; matrix products, arithmetic and copies ran while one was open for 82% -> 11% of each run, Pallas kernels for 0% -> 0%
where the time goes in v1:
time: 145 us; the launch traced here: 144 us
  waiting for transfers between devices  55.8 us (38%)
  local copies, waits for them, and re-layouts  23.5 us (16%)
  starting transfers between devices  20.8 us (14%)
  other arithmetic  18.4 us (13%)
  between operations  11.5 us (8%)
  Pallas kernels  9.07 us (6%)
  blocking collectives  5.35 us (4%)
    ppermute x3, waiting for transfers between devices, extended_2(): before = lax.ppermute(last, axis, up)  45.1 us
    concatenate x1, other arithmetic, extended_2(): array = jnp.concatenate([before, array, after], axis=dim)  13.7 us
    ppermute x3, starting transfers between devices, extended_2(): before = lax.ppermute(last, axis, up)  12.7 us
    pallas_call x1, Pallas kernels, coarse_parts(): pl.pallas_call(patch_kernel, out_shape=(jax.ShapeDtypeStruct((slot_count,...  9.07 us
    ppermute x3, waiting for transfers between devices, extended_2(): after = lax.ppermute(first, axis, down)  8.89 us
    all_to_all x1, blocking collectives, local(): lax.all_to_all(blocks, 'gz', split_axis=0, concat_axis=0, tiled=True)  5.35 us
    unnamed x19, local copies, waits for them, and re-layouts  4.86 us
    ppermute x3, starting transfers between devices, extended_2(): after = lax.ppermute(first, axis, down)  4.67 us
  transfers between devices with their start and end apart: 7, of which 7 were waited for; matrix products, arithmetic and copies ran while one was open for 11% of the time, Pallas kernels for 0%

profile of v1, /device:TPU:1, one launch (start us, length us, event | category | flops | bytes accessed | tf_op | source)
XLA Modules:
  0.0 144.3 jit_solution(9252842405304565057)
XLA Ops:
  0.6 1.8 %fusion.7 = (bf16[4,24,24,256]{3,2,1,0:T(8,128)(2,1)S(1)}, bf16[4,24,24,256]{3,2,1,0:T(8,128)(2,1)S(1)}) fusion(bf16[24,24,24,256]{3,2,1,0:T(8,128)(2,1)} %param.8), kind=kLoop, calls=%fused_computation.43 | loop fusion | bytes 4718592 | tf_op jit(solution)/shard_map/slice | solution.py:193
  2.4 4.5 %collective-permute-start = (bf16[4,24,24,256]{3,2,1,0:T(8,128)(2,1)S(1)}, bf16[4,24,24,256]{3,2,1,0:T(8,128)(2,1)S(1)}, u32[]{:S(2)}, u32[]{:S(2)}) collective-permute-start(bf16[4,24,24,256]{3,2,1,0:T(8,128)(2,1)S(1)} %get-tuple-element.21), channel_id=1, source_target_pairs={{0,8},{8,16},{16,24},{1,9},{9,17},{17,25},{2,10},{10,18},{18,26},{... | collective-permute-start | bytes 3538952 | tf_op jit(solution)/shard_map/ppermute | solution.py:194
  6.9 1.9 %collective-permute-start.1 = (bf16[4,24,24,256]{3,2,1,0:T(8,128)(2,1)S(1)}, bf16[4,24,24,256]{3,2,1,0:T(8,128)(2,1)S(1)}, u32[]{:S(2)}, u32[]{:S(2)}) collective-permute-start(bf16[4,24,24,256]{3,2,1,0:T(8,128)(2,1)S(1)} %get-tuple-element.20), channel_id=1, source_target_pairs={{8,0},{16,8},{24,16},{9,1},{17,9},{25,17},{10,2},{18,10},{26,18},{... | collective-permute-start | bytes 3538952 | tf_op jit(solution)/shard_map/ppermute | solution.py:195
  8.9 11.2 %collective-permute-done = bf16[4,24,24,256]{3,2,1,0:T(8,128)(2,1)S(1)} collective-permute-done((bf16[4,24,24,256]{3,2,1,0:T(8,128)(2,1)S(1)}, bf16[4,24,24,256]{3,2,1,0:T(8,128)(2,1)S(1)}, u32[]{:S(2)}, u32[]{:S(2)}) %collective-permute-start) | collective-permute-done | bytes 1179680 | tf_op jit(solution)/shard_map/ppermute | solution.py:194
  20.1 3.5 %constant_dynamic-update-slice_fusion.1 = bf16[32,24,24,256]{3,2,1,0:T(8,128)(2,1)S(1)} fusion(bf16[32,24,24,256]{3,2,1,0:T(8,128)(2,1)S(1)} %constant_dynamic-update-slice_fusion.2, bf16[24,24,24,256]{3,2,1,0:T(8,128)(2,1)} %param.8), kind=kLoop, calls=%fused_computation.15 | loop fusion | bytes 14155776
  23.7 1.1 collective-permute-done.1
  25.1 3.3 %collective-permute-start.2 = (bf16[32,4,24,256]{3,2,1,0:T(8,128)(2,1)S(1)}, bf16[32,4,24,256]{3,2,1,0:T(8,128)(2,1)S(1)}, u32[]{:S(2)}, u32[]{:S(2)}) collective-permute-start(bf16[32,4,24,256]{3,2,1,0:T(8,128)(2,1)S(1)} %get-tuple-element.18), channel_id=1, source_target_pairs={{0,2},{2,4},{4,6},{1,3},{3,5},{5,7},{8,10},{10,12},{12,14},{9,11},... | collective-permute-start | bytes 4718600 | tf_op jit(solution)/shard_map/ppermute | solution.py:194
  28.4 1.3 collective-permute-start.3
  29.7 20.3 %collective-permute-done.2 = bf16[32,4,24,256]{3,2,1,0:T(8,128)(2,1)S(1)} collective-permute-done((bf16[32,4,24,256]{3,2,1,0:T(8,128)(2,1)S(1)}, bf16[32,4,24,256]{3,2,1,0:T(8,128)(2,1)S(1)}, u32[]{:S(2)}, u32[]{:S(2)}) %collective-permute-start.2) | collective-permute-done | bytes 1572896 | tf_op jit(solution)/shard_map/ppermute | solution.py:194
  50.0 4.2 %collective-permute-done.3 = bf16[32,4,24,256]{3,2,1,0:T(8,128)(2,1)S(1)} collective-permute-done((bf16[32,4,24,256]{3,2,1,0:T(8,128)(2,1)S(1)}, bf16[32,4,24,256]{3,2,1,0:T(8,128)(2,1)S(1)}, u32[]{:S(2)}, u32[]{:S(2)}) %collective-permute-start.3) | collective-permute-done | bytes 1572896 | tf_op jit(solution)/shard_map/ppermute | solution.py:195
  54.2 2.6 %pad_maximum_fusion.3 = (bf16[32,32,4,256]{3,2,1,0:T(4,128)(2,1)S(1)}, bf16[32,32,4,256]{3,2,1,0:T(4,128)(2,1)S(1)}) fusion(bf16[32,4,24,256]{3,2,1,0:T(8,128)(2,1)S(1)} %collective-permute-done.3, bf16[32,24,24,256]{3,2,1,0:T(8,128)(2,1)S(1)} %constant_dynamic-update-slice_fusion, bf16[32,4,24,256]{3,2,1,0:T(8,128)(2,1)S(1)} %collective-permute-done.2), kind=kLoop, calls=%fused_computation.3 | loop fusion | flops 12582912 | bytes 16777216 | tf_op jit(solution)/shard_map/slice | solution.py:192
  56.8 1.8 %copy.73 = bf16[32,32,4,256]{3,1,2,0:T(8,128)(2,1)} copy(bf16[32,32,4,256]{3,2,1,0:T(4,128)(2,1)S(1)} %get-tuple-element.16) | data formatting | bytes 4194304 | tf_op jit(solution)/shard_map/slice | solution.py:192
  58.6 4.9 %collective-permute-start.4 = (bf16[32,32,4,256]{3,1,2,0:T(8,128)(2,1)}, bf16[32,32,4,256]{3,1,2,0:T(8,128)(2,1)}, u32[]{:S(2)}, u32[]{:S(2)}) collective-permute-start(bf16[32,32,4,256]{3,1,2,0:T(8,128)(2,1)} %copy.73), channel_id=1, source_target_pairs={{0,1},{2,3},{4,5},{6,7},{8,9},{10,11},{12,13},{14,15},{16,17},{18,... | collective-permute-start | bytes 6291464 | tf_op jit(solution)/shard_map/ppermute | solution.py:194
  63.4 1.8 %copy.74 = bf16[32,32,4,256]{3,1,2,0:T(8,128)(2,1)} copy(bf16[32,32,4,256]{3,2,1,0:T(4,128)(2,1)S(1)} %get-tuple-element.17) | data formatting | bytes 4194304 | tf_op jit(solution)/shard_map/slice | solution.py:193
  65.2 1.5 %collective-permute-start.5 = (bf16[32,32,4,256]{3,1,2,0:T(8,128)(2,1)}, bf16[32,32,4,256]{3,1,2,0:T(8,128)(2,1)}, u32[]{:S(2)}, u32[]{:S(2)}) collective-permute-start(bf16[32,32,4,256]{3,1,2,0:T(8,128)(2,1)} %copy.74), channel_id=1, source_target_pairs={{1,0},{3,2},{5,4},{7,6},{9,8},{11,10},{13,12},{15,14},{17,16},{19,... | collective-permute-start | bytes 6291464 | tf_op jit(solution)/shard_map/ppermute | solution.py:195
  66.7 1.4 fusion.8
  78.5 0.8 select_reduce_fusion
  80.2 0.4 slice_reduce_fusion.3
  82.6 13.7 %collective-permute-done.4 = bf16[32,32,4,256]{3,1,2,0:T(8,128)(2,1)} collective-permute-done((bf16[32,32,4,256]{3,1,2,0:T(8,128)(2,1)}, bf16[32,32,4,256]{3,1,2,0:T(8,128)(2,1)}, u32[]{:S(2)}, u32[]{:S(2)}) %collective-permute-start.4) | collective-permute-done | bytes 2097184 | tf_op jit(solution)/shard_map/ppermute | solution.py:194
  96.3 3.6 %copy.75 = bf16[32,32,4,256]{3,2,1,0:T(4,128)(2,1)S(1)} copy(bf16[32,32,4,256]{3,1,2,0:T(8,128)(2,1)} %collective-permute-done.4) | data formatting | bytes 4194304 | tf_op jit(solution)/shard_map/ppermute | solution.py:194
  99.8 3.6 %collective-permute-done.5 = bf16[32,32,4,256]{3,1,2,0:T(8,128)(2,1)} collective-permute-done((bf16[32,32,4,256]{3,1,2,0:T(8,128)(2,1)}, bf16[32,32,4,256]{3,1,2,0:T(8,128)(2,1)}, u32[]{:S(2)}, u32[]{:S(2)}) %collective-permute-start.5) | collective-permute-done | bytes 2097184 | tf_op jit(solution)/shard_map/ppermute | solution.py:195
  103.5 3.6 %copy.76 = bf16[32,32,4,256]{3,2,1,0:T(4,128)(2,1)S(1)} copy(bf16[32,32,4,256]{3,1,2,0:T(8,128)(2,1)} %collective-permute-done.5) | data formatting | bytes 4194304 | tf_op jit(solution)/shard_map/ppermute | solution.py:195
  107.0 13.7 %pad_maximum_fusion = bf16[32,32,32,256]{3,2,1,0:T(8,128)(2,1)S(1)} fusion(bf16[32,32,4,256]{3,2,1,0:T(4,128)(2,1)S(1)} %copy.76, bf16[32,4,24,256]{3,2,1,0:T(8,128)(2,1)S(1)} %collective-permute-done.3, bf16[32,24,24,256]{3,2,1,0:T(8,128)(2,1)} %copy-done.1, bf16[32,4,24,256]{3,2,1,0:T(8,128)(2,1)S(1)} %collective-permute-done.2, ...), kind=kLoop, calls=%fused_computation | loop fusion | flops 83886080 | bytes 33554432 | tf_op jit(solution)/shard_map/concatenate | solution.py:196
  120.8 0.4 constant_dynamic-slice_fusion.2
  121.4 9.1 %patches.1 = (f32[4,64,64]{2,1,0:T(8,128)S(1)}, f32[4,64,256]{2,1,0:T(8,128)}) custom-call(s32[4]{0:T(128)S(1)} %multiply_add_fusion.slot_ref, f32[30]{0:T(128)S(1)} %copy-done, bf16[2,3,256,4]{3,2,1,0:T(8,128)(2,1)S(1)} %pad_maximum_fusion.5.dofs_ref, bf16[4,512,256]{2,1,0:T(8,128)(2,1)S(1)} %pad_maximum_fusion.4.rows_ref), custom_call_target="tpu_custom_call" | custom-call | flops 1000000000 | bytes 2097152 | tf_op jit(solution)/shard_map/patches/pallas_call | solution.py:174
  130.6 5.3 %all_to_all.10 = f32[2,1,8192]{2,1,0:T(1,128)S(1)} all-to-all(f32[2,1,8192]{2,1,0:T(1,128)S(1)} %reshape.290), channel_id=1, replica_groups=mesh['gx'=4,'gy'=4,'gz'=2] {'gz'}, dimensions={0} | all-to-all | bytes 131072 | tf_op jit(solution)/shard_map/all_to_all | solution.py:225
  136.0 3.4 %all-to-all-start.1 = ((f32[4,64,256]{2,1,0:T(8,128)}), f32[4,64,256]{2,1,0:T(8,128)S(1)}, u32[]{:S(2)}, u32[]{:S(2)}) async-start(f32[4,64,256]{2,1,0:T(8,128)} %get-tuple-element.5), calls=%async_computation.1 | async-start | bytes 524288 | tf_op jit(solution)/shard_map/all_to_all | solution.py:226
  139.4 0.5 broadcast.176
  139.9 0.8 reduce.12
  140.9 0.7 reshape.281
  141.7 1.8 %all-to-all-done.1 = f32[4,64,256]{2,1,0:T(8,128)S(1)} async-done(((f32[4,64,256]{2,1,0:T(8,128)}), f32[4,64,256]{2,1,0:T(8,128)S(1)}, u32[]{:S(2)}, u32[]{:S(2)}) %all-to-all-start.1) | async-done | bytes 262176 | tf_op jit(solution)/shard_map/all_to_all | solution.py:226
  143.4 0.9 copy.81
  (45 shorter events, 3.6 us)
Async XLA Ops:
  2.4 17.6 %collective-permute-start = (bf16[4,24,24,256]{3,2,1,0:T(8,128)(2,1)S(1)}, bf16[4,24,24,256]{3,2,1,0:T(8,128)(2,1)S(1)}, u32[]{:S(2)}, u32[]{:S(2)}) collective-permute-start(bf16[4,24,24,256]{3,2,1,0:T(8,128)(2,1)S(1)} %get-tuple-element.21), channel_id=1, source_target_pairs={{0,8},{8,16},{16,24},{1,9},{9,17},{17,25},{2,10},{10,18},{18,26},{... | collective-permute-start | bytes 3538952 | tf_op jit(solution)/shard_map/ppermute | solution.py:194
  6.9 17.8 %collective-permute-start.1 = (bf16[4,24,24,256]{3,2,1,0:T(8,128)(2,1)S(1)}, bf16[4,24,24,256]{3,2,1,0:T(8,128)(2,1)S(1)}, u32[]{:S(2)}, u32[]{:S(2)}) collective-permute-start(bf16[4,24,24,256]{3,2,1,0:T(8,128)(2,1)S(1)} %get-tuple-element.20), channel_id=1, source_target_pairs={{8,0},{16,8},{24,16},{9,1},{17,9},{25,17},{10,2},{18,10},{26,18},{... | collective-permute-start | bytes 3538952 | tf_op jit(solution)/shard_map/ppermute | solution.py:195
  24.8 31.9 %copy-start.1 = (bf16[32,24,24,256]{3,2,1,0:T(8,128)(2,1)}, bf16[32,24,24,256]{3,2,1,0:T(8,128)(2,1)S(1)}, u32[]{:S(2)}) copy-start(bf16[32,24,24,256]{3,2,1,0:T(8,128)(2,1)S(1)} %constant_dynamic-update-slice_fusion) | copy-start | bytes 28311556
  25.1 24.9 %collective-permute-start.2 = (bf16[32,4,24,256]{3,2,1,0:T(8,128)(2,1)S(1)}, bf16[32,4,24,256]{3,2,1,0:T(8,128)(2,1)S(1)}, u32[]{:S(2)}, u32[]{:S(2)}) collective-permute-start(bf16[32,4,24,256]{3,2,1,0:T(8,128)(2,1)S(1)} %get-tuple-element.18), channel_id=1, source_target_pairs={{0,2},{2,4},{4,6},{1,3},{3,5},{5,7},{8,10},{10,12},{12,14},{9,11},... | collective-permute-start | bytes 4718600 | tf_op jit(solution)/shard_map/ppermute | solution.py:194
  28.4 25.8 %collective-permute-start.3 = (bf16[32,4,24,256]{3,2,1,0:T(8,128)(2,1)S(1)}, bf16[32,4,24,256]{3,2,1,0:T(8,128)(2,1)S(1)}, u32[]{:S(2)}, u32[]{:S(2)}) collective-permute-start(bf16[32,4,24,256]{3,2,1,0:T(8,128)(2,1)S(1)} %get-tuple-element.19), channel_id=1, source_target_pairs={{2,0},{4,2},{6,4},{3,1},{5,3},{7,5},{10,8},{12,10},{14,12},{11,9},... | collective-permute-start | bytes 4718600 | tf_op jit(solution)/shard_map/ppermute | solution.py:195
  56.8 21.8 %copy-start.5 = (bf16[256]{0:T(256)(128)(2,1)S(1)}, bf16[256]{0:T(256)(128)(2,1)}, u32[]{:S(2)}) copy-start(bf16[256]{0:T(256)(128)(2,1)} %param.9) | copy-start | bytes 1540
  56.8 21.8 %copy-start.3 = (s32[4,512]{1,0:T(4,128)S(1)}, s32[4,512]{1,0:T(4,128)}, u32[]{:S(2)}) copy-start(s32[4,512]{1,0:T(4,128)} %param.10) | copy-start | bytes 24580
  56.8 23.3 %copy-start.2 = (s32[4,512]{1,0:T(4,128)S(1)}, s32[4,512]{1,0:T(4,128)}, u32[]{:S(2)}) copy-start(s32[4,512]{1,0:T(4,128)} %param.12) | copy-start | bytes 24580
  56.8 24.0 %copy-start.4 = (bf16[4,512]{1,0:T(4,128)(2,1)S(1)}, bf16[4,512]{1,0:T(4,128)(2,1)}, u32[]{:S(2)}) copy-start(bf16[4,512]{1,0:T(4,128)(2,1)} %param.13) | copy-start | bytes 12292
  56.8 25.5 %copy-start.6 = (s32[4]{0:T(128)S(1)}, s32[4]{0:T(128)}, u32[]{:S(2)}) copy-start(s32[4]{0:T(128)} %param.14) | copy-start | bytes 52
  58.6 37.7 %collective-permute-start.4 = (bf16[32,32,4,256]{3,1,2,0:T(8,128)(2,1)}, bf16[32,32,4,256]{3,1,2,0:T(8,128)(2,1)}, u32[]{:S(2)}, u32[]{:S(2)}) collective-permute-start(bf16[32,32,4,256]{3,1,2,0:T(8,128)(2,1)} %copy.73), channel_id=1, source_target_pairs={{0,1},{2,3},{4,5},{6,7},{8,9},{10,11},{12,13},{14,15},{16,17},{18,... | collective-permute-start | bytes 6291464 | tf_op jit(solution)/shard_map/ppermute | solution.py:194
  65.2 38.3 %collective-permute-start.5 = (bf16[32,32,4,256]{3,1,2,0:T(8,128)(2,1)}, bf16[32,32,4,256]{3,1,2,0:T(8,128)(2,1)}, u32[]{:S(2)}, u32[]{:S(2)}) collective-permute-start(bf16[32,32,4,256]{3,1,2,0:T(8,128)(2,1)} %copy.74), channel_id=1, source_target_pairs={{1,0},{3,2},{5,4},{7,6},{9,8},{11,10},{13,12},{15,14},{17,16},{19,... | collective-permute-start | bytes 6291464 | tf_op jit(solution)/shard_map/ppermute | solution.py:195
  120.8 0.7 copy-start
  136.0 7.5 %all-to-all-start.1 = ((f32[4,64,256]{2,1,0:T(8,128)}), f32[4,64,256]{2,1,0:T(8,128)S(1)}, u32[]{:S(2)}, u32[]{:S(2)}) async-start(f32[4,64,256]{2,1,0:T(8,128)} %get-tuple-element.5), calls=%async_computation.1 | async-start | bytes 524288 | tf_op jit(solution)/shard_map/all_to_all | solution.py:226

commit v2 on v1

--- a/solution.py
+++ b/solution.py
@@ -61,7 +61,7 @@
         new[x] = current + weight * (gate[x] * total + bias[x] - current)
 
 
-def patch_kernel(slot_ref, omega_ref, dofs_ref, rows_ref, block_ref, part_ref,
+def patch_kernel(slot_ref, omega_ref, dofs_ref, rows_ref, out_ref,
                  red, black, bias_r, bias_k, gate_r, gate_k, root_r, root_k):
     patches = rows_ref.shape[0]
     lanes = patches * M
@@ -119,9 +119,9 @@
     coarse = response.astype(jnp.bfloat16)
     fine = (response - coarse.astype(jnp.float32)).astype(jnp.bfloat16)
     coarse, fine = coarse.T, fine.T
-    if part_ref.shape[0] > patches:
-        block_ref[...] = jnp.zeros(block_ref.shape, jnp.float32)
-        part_ref[...] = jnp.zeros(part_ref.shape, jnp.float32)
+    width = rows_ref.shape[-1]
+    if out_ref.shape[0] > patches:
+        out_ref[...] = jnp.zeros(out_ref.shape, jnp.float32)
     identity = jnp.where(
         lax.broadcasted_iota(jnp.int32, (M, M), 0) == lax.broadcasted_iota(jnp.int32, (M, M), 1), 1.0, 0.0)
     p0, p1, p2 = start_polynomial()
@@ -145,8 +145,8 @@
                      + jnp.dot(fine[mine], rows, preferred_element_type=jnp.float32))
         down, across = scales[p]
         block = inverse[p] * down * across
-        block_ref[slot_ref[p]] = block
-        part_ref[slot_ref[p]] = exact_dot(block, projected)
+        out_ref[slot_ref[p], :, width:] = block
+        out_ref[slot_ref[p], :, :width] = exact_dot(block, projected)
 
 
 def reduce_weight(dofs_ref, spot, color, x, lanes):
@@ -173,10 +173,9 @@
     grid = pltpu.VMEM((BOX, HALF, BOX, lanes), jnp.float32)
     return pl.pallas_call(
         patch_kernel,
-        out_shape=(jax.ShapeDtypeStruct((slot_count, M, M), jnp.float32),
-                   jax.ShapeDtypeStruct((slot_count, M, patch_rows.shape[-1]), jnp.float32)),
+        out_shape=jax.ShapeDtypeStruct((slot_count, M, patch_rows.shape[-1] + M), jnp.float32),
         in_specs=[smem, smem, vmem, vmem],
-        out_specs=(vmem, vmem),
+        out_specs=vmem,
         scratch_shapes=[grid] * 8,
         compiler_params=pltpu.CompilerParams(vmem_limit_bytes=40 * 1024 * 1024),
         cost_estimate=pl.CostEstimate(flops=10**9, bytes_accessed=2**21, transcendentals=0),
@@ -184,30 +183,65 @@
     )(target_slot, omega, dofs, patch_rows)
 
 
-def extended_2(array, sides, width):
-    for axis, dim in sides:
-        size, length = (lax.axis_size(axis), array.shape[dim])
-        up = [(i, (i + 1) % size) for i in range(size - 1)]
-        down = [(j, i) for i, j in up]
-        last = lax.slice_in_dim(array, length - width, length, axis=dim)
-        first = lax.slice_in_dim(array, 0, width, axis=dim)
-        before = lax.ppermute(last, axis, up)
-        after = lax.ppermute(first, axis, down)
-        array = jnp.concatenate([before, array, after], axis=dim)
-    return array
+def up_down(axis):
+    size = lax.axis_size(axis)
+    up = [(i, i + 1) for i in range(size - 1)]
+    return up, [(j, i) for i, j in up]
+
+
+def edges(array, dim):
+    length = array.shape[dim]
+    return lax.slice_in_dim(array, length - HW, length, axis=dim), lax.slice_in_dim(array, 0, HW, axis=dim)
+
+
+def exchanged(last, first, axis):
+    up, down = up_down(axis)
+    return lax.ppermute(last, axis, up), lax.ppermute(first, axis, down)
+
+
+def widened(array, before, after, dim):
+    pad = [(HW, HW, 0) if d == dim else (0, 0, 0) for d in range(array.ndim)]
+    wide = lax.pad(array, jnp.zeros((), array.dtype), pad)
+    wide = lax.dynamic_update_slice_in_dim(wide, before, 0, axis=dim)
+    return lax.dynamic_update_slice_in_dim(wide, after, array.shape[dim] + HW, axis=dim)
+
+
+def boxes(fine_rhs, localization):
+    extent = [n + 2 * HW for n in fine_rhs.shape[:3]]
+    corner = localization[:, 0]
+    lower, upper = exchanged(corner, corner, "gz")
+    before, after = exchanged(*edges(fine_rhs, 0), "gx")
+    y_last, y_first = edges(fine_rhs, 1)
+    last_y = jnp.concatenate([edges(before, 1)[0], y_last, edges(after, 1)[0]], axis=0)
+    first_y = jnp.concatenate([edges(before, 1)[1], y_first, edges(after, 1)[1]], axis=0)
+    y_before, y_after = exchanged(last_y, first_y, "gy")
+    wide = widened(widened(fine_rhs, before, after, 0), y_before, y_after, 1)
+
+    def window(source, first):
+        at = (first // (extent[1] * extent[2]), first // extent[2] % extent[1], 0, 0)
+        return lax.dynamic_slice(source, at, (BOX, BOX) + source.shape[2:])
+
+    count = localization.shape[0]
+    rising = [p for p in range(count) if p != 1]
+    falling = [p for p in range(count) if p != 0]
+    z_last, z_first = edges(wide, 2)
+    sent_up = jnp.stack([window(z_last, upper[p]) for p in rising])
+    sent_down = jnp.stack([window(z_first, lower[p]) for p in falling])
+    z_before, z_after = exchanged(sent_up, sent_down, "gz")
+    nothing = jnp.zeros((BOX, BOX, HW, fine_rhs.shape[-1]), fine_rhs.dtype)
+    rows = []
+    for p in range(count):
+        low = z_before[rising.index(p)] if p in rising else nothing
+        top = z_after[falling.index(p)] if p in falling else nothing
+        column = jnp.concatenate([low, window(wide, corner[p]), top], axis=2)
+        box = lax.dynamic_slice_in_dim(column, corner[p] % extent[2], BOX, axis=2)
+        rows.append(box.reshape(PATCH, -1))
+    return jnp.stack(rows)
 
 
 def local(fine_rhs, coef_table, coef_ids, localization, patch_mask, measure_weights, owners):
-    extended = extended_2(fine_rhs, (("gx", 0), ("gy", 1), ("gz", 2)), HW)
     patch_count = localization.shape[0]
-    extent = extended.shape[:3]
-    rows = []
-    for p in range(patch_count):
-        first = localization[p, 0]
-        corner = (first // (extent[1] * extent[2]), first // extent[2] % extent[1], first % extent[2], 0)
-        box = lax.dynamic_slice(extended, corner, (BOX, BOX, BOX, extended.shape[-1]))
-        rows.append(box.reshape(PATCH, -1))
-    patch_rows = jnp.stack(rows)
+    patch_rows = boxes(fine_rhs, localization)
     table_hits = (
         coef_ids[:, :, None] == jnp.arange(coef_table.shape[0], dtype=jnp.int32)[None, None, :]
     )
@@ -221,10 +255,10 @@
     earlier = jnp.arange(patch_count)[:, None] > jnp.arange(patch_count)[None, :]
     slot_rank = jnp.sum(jnp.where(same & earlier, 1, 0), axis=1).astype(jnp.int32)
     target_slot = owners * capacity + slot_rank
-    blocks, parts = coarse_parts(target_slot, slot_count, coefficient, patch_mask, measure_weights, patch_rows)
-    blocks = lax.all_to_all(blocks, "gz", split_axis=0, concat_axis=0, tiled=True)
-    parts = lax.all_to_all(parts, "gz", split_axis=0, concat_axis=0, tiled=True)
-    return (blocks.reshape(slot_count, -1), parts.reshape(slot_count, -1))
+    results = coarse_parts(target_slot, slot_count, coefficient, patch_mask, measure_weights, patch_rows)
+    results = lax.all_to_all(results, "gz", split_axis=0, concat_axis=0, tiled=True)
+    width = fine_rhs.shape[-1]
+    return (results[:, :, width:].reshape(slot_count, -1), results[:, :, :width].reshape(slot_count, -1))
 
 
 def solution(mesh):

time: 145 us -> 141 us (0.972)
  the two profiles are of different devices: /device:TPU:1 before, /device:TPU:0 now
where the time goes in v2:
time: 141 us; the launch traced here: 140 us
  local copies, waits for them, and re-layouts  48.1 us (34%)
  between operations  27.5 us (20%)
  starting transfers between devices  23.3 us (17%)
  waiting for transfers between devices  16.7 us (12%)
  blocking collectives  9.43 us (7%)
  Pallas kernels  8.13 us (6%)
  other arithmetic  6.87 us (5%)
    ppermute x8, starting transfers between devices, exchanged(): return (lax.ppermute(last, axis, up), lax.ppermute(first, axis, down))  23.3 us
    ppermute x8, waiting for transfers between devices, exchanged(): return (lax.ppermute(last, axis, up), lax.ppermute(first, axis, down))  16.7 us
    pad x2, local copies, waits for them, and re-layouts, widened(): wide = lax.pad(array, jnp.zeros((), array.dtype), pad)  13.3 us
    all_to_all x1, blocking collectives, local(): lax.all_to_all(results, 'gz', split_axis=0, concat_axis=0, tiled=True)  9.43 us
    pallas_call x1, Pallas kernels, coarse_parts(): pl.pallas_call(patch_kernel, out_shape=jax.ShapeDtypeStruct((slot_count,...  8.13 us
    squeeze x6, local copies, waits for them, and re-layouts, two_colors(): first, second = (cells[:, :, :, 0], cells[:, :, :, 1])  6.8 us
    slice x5, local copies, waits for them, and re-layouts, edges(): lax.slice_in_dim(array, 0, HW, axis=dim)  6.31 us
    slice x3, local copies, waits for them, and re-layouts, two_colors(): first, second = (cells[:, :, :, 0], cells[:, :, :, 1])  5.8 us
  transfers between devices with their start and end apart: 8, of which 4 were waited for; matrix products, arithmetic and copies ran while one was open for 32% of the time, Pallas kernels for 0%

profile of v2, /device:TPU:0, one launch (start us, length us, event | category | flops | bytes accessed | tf_op | source)
XLA Modules:
  0.0 140.0 jit_solution(4518648586019385952)
XLA Ops:
  0.6 2.8 %fusion.16 = (bf16[4,24,24,256]{3,2,1,0:T(8,128)(2,1)S(1)}, bf16[4,24,24,256]{3,2,1,0:T(8,128)(2,1)}) fusion(bf16[24,24,24,256]{3,2,1,0:T(8,128)(2,1)} %param.8), kind=kLoop, calls=%fused_computation.79 | loop fusion | bytes 4718592 | tf_op jit(solution)/shard_map/slice | solution.py:194
  3.4 2.4 %collective-permute-start = (bf16[4,24,24,256]{3,2,1,0:T(8,128)(2,1)}, bf16[4,24,24,256]{3,2,1,0:T(8,128)(2,1)S(1)}, u32[]{:S(2)}, u32[]{:S(2)}) collective-permute-start(bf16[4,24,24,256]{3,2,1,0:T(8,128)(2,1)} %get-tuple-element.17), channel_id=1, source_target_pairs={{0,8},{8,16},{16,24},{1,9},{9,17},{17,25},{2,10},{10,18},{18,26},{... | collective-permute-start | bytes 3538952 | tf_op jit(solution)/shard_map/ppermute | solution.py:199
  6.5 1.3 collective-permute-start.4
  7.8 5.5 %collective-permute-start.6 = (s32[4]{0:T(128)}, s32[4]{0:T(128)}, u32[]{:S(2)}, u32[]{:S(2)}) collective-permute-start(s32[4]{0:T(128)} %slice_reduce_fusion.6), channel_id=1, source_target_pairs={{0,1},{2,3},{4,5},{6,7},{8,9},{10,11},{12,13},{14,15},{16,17},{18,... | collective-permute-start | bytes 56 | tf_op jit(solution)/shard_map/ppermute | solution.py:199
  13.3 1.3 collective-permute-start.1
  25.9 7.6 %pad.6 = bf16[32,24,24,256]{3,2,1,0:T(8,128)(2,1)} pad(bf16[24,24,24,256]{3,2,1,0:T(8,128)(2,1)} %param.8, bf16[]{:T(256)} %constant.239.clone.1), padding=4_4x0_0x0_0x0_0 | pad | bytes 16515074 | tf_op jit(solution)/shard_map/pad | solution.py:204
  35.0 1.9 %slice_reduce_fusion.5 = (bf16[4,8,4,8]{3,2,1,0:T(4,128)(2,1)}, bf16[4,8,4,8]{3,2,1,0:T(4,128)(2,1)}) fusion(bf16[4,8,4,2,8]{4,3,2,1,0:T(2,128)(2,1)} %convert_element_type.15), kind=kLoop, calls=%fused_computation.46 | loop fusion | bytes 8192 | tf_op jit(solution)/shard_map/slice | solution.py:161
  40.1 1.9 %slice_reduce_fusion.3 = (bf16[4,8,4,8]{3,2,1,0:T(4,128)(2,1)}, bf16[4,8,4,8]{3,2,1,0:T(4,128)(2,1)}) fusion(bf16[4,8,4,2,8]{4,3,2,1,0:T(2,128)(2,1)} %reshape.287), kind=kLoop, calls=%fused_computation.44 | loop fusion | bytes 8192 | tf_op jit(solution)/shard_map/slice | solution.py:161
  42.9 1.4 squeeze.76
  44.3 1.4 %reshape.288 = bf16[4,8,4,2,8]{4,3,2,1,0:T(2,128)(2,1)} reshape(bf16[4,512]{1,0:T(4,128)(2,1)} %param.13) | data formatting | bytes 8192 | tf_op jit(solution)/shard_map/reshape | solution.py:159
  45.7 1.9 %slice_reduce_fusion.1 = (bf16[4,8,4,8]{3,2,1,0:T(4,128)(2,1)}, bf16[4,8,4,8]{3,2,1,0:T(4,128)(2,1)}) fusion(bf16[4,8,4,2,8]{4,3,2,1,0:T(2,128)(2,1)} %reshape.288), kind=kLoop, calls=%fused_computation.42 | loop fusion | bytes 8192 | tf_op jit(solution)/shard_map/slice | solution.py:161
  47.7 1.4 squeeze.77
  49.1 1.4 %squeeze.78 = bf16[1,4,256]{2,1,0:T(4,128)(2,1)} reshape(bf16[4,8,4,8]{3,2,1,0:T(4,128)(2,1)} %get-tuple-element.7) | data formatting | bytes 4096 | tf_op jit(solution)/shard_map/squeeze | solution.py:161
  50.5 1.8 %fusion.15 = (bf16[24,4,24,256]{3,2,1,0:T(8,128)(2,1)S(1)}, bf16[24,4,24,256]{3,2,1,0:T(8,128)(2,1)S(1)}) fusion(bf16[24,24,24,256]{3,2,1,0:T(8,128)(2,1)} %param.8), kind=kLoop, calls=%fused_computation.78 | loop fusion | bytes 4718592 | tf_op jit(solution)/shard_map/slice | solution.py:194
  52.4 1.4 pad_maximum_fusion
  53.7 5.5 %collective-permute-start.2 = (bf16[32,4,24,256]{3,2,1,0:T(8,128)(2,1)}, bf16[32,4,24,256]{3,2,1,0:T(8,128)(2,1)}, u32[]{:S(2)}, u32[]{:S(2)}) collective-permute-start(bf16[32,4,24,256]{3,2,1,0:T(8,128)(2,1)} %pad_maximum_fusion), channel_id=1, source_target_pairs={{0,2},{2,4},{4,6},{1,3},{3,5},{5,7},{8,10},{10,12},{12,14},{9,11},... | collective-permute-start | bytes 4718600 | tf_op jit(solution)/shard_map/ppermute | solution.py:199
  59.2 1.4 pad_maximum_fusion.1
  60.6 1.3 collective-permute-start.3
  62.9 1.3 fusion.21
  72.1 1.3 fusion.20
  83.6 5.7 %pad.7 = bf16[32,32,24,256]{3,2,1,0:T(8,128)(2,1)S(1)} pad(bf16[32,24,24,256]{3,2,1,0:T(8,128)(2,1)} %constant_dynamic-update-slice_fusion.2, bf16[]{:T(256)} %constant.239.clone.1), padding=0_0x4_4x0_0x0_0 | pad | bytes 22020098 | tf_op jit(solution)/shard_map/pad | solution.py:204
  89.4 3.0 %collective-permute-done.2 = bf16[32,4,24,256]{3,2,1,0:T(8,128)(2,1)} collective-permute-done((bf16[32,4,24,256]{3,2,1,0:T(8,128)(2,1)}, bf16[32,4,24,256]{3,2,1,0:T(8,128)(2,1)}, u32[]{:S(2)}, u32[]{:S(2)}) %collective-permute-start.2) | collective-permute-done | bytes 1572896 | tf_op jit(solution)/shard_map/ppermute | solution.py:199
  92.4 1.5 %constant_dynamic-update-slice_fusion.1 = bf16[32,32,24,256]{3,2,1,0:T(8,128)(2,1)S(1)} fusion(bf16[32,32,24,256]{3,2,1,0:T(8,128)(2,1)S(1)} %pad.7, bf16[32,4,24,256]{3,2,1,0:T(8,128)(2,1)} %collective-permute-done.2), kind=kLoop, calls=%fused_computation.52 | loop fusion | bytes 3145728 | tf_op jit(solution)/shard_map/dynamic_update_slice | solution.py:205
  93.9 5.7 %collective-permute-done.3 = bf16[32,4,24,256]{3,2,1,0:T(8,128)(2,1)} collective-permute-done((bf16[32,4,24,256]{3,2,1,0:T(8,128)(2,1)}, bf16[32,4,24,256]{3,2,1,0:T(8,128)(2,1)}, u32[]{:S(2)}, u32[]{:S(2)}) %collective-permute-start.3) | collective-permute-done | bytes 1572896 | tf_op jit(solution)/shard_map/ppermute | solution.py:199
  99.6 1.5 %constant_dynamic-update-slice_fusion = bf16[32,32,24,256]{3,2,1,0:T(8,128)(2,1)S(1)} fusion(bf16[32,32,24,256]{3,2,1,0:T(8,128)(2,1)S(1)} %constant_dynamic-update-slice_fusion.1, bf16[32,4,24,256]{3,2,1,0:T(8,128)(2,1)} %collective-permute-done.3), kind=kLoop, calls=%fused_computation.51 | loop fusion | bytes 3145728 | tf_op jit(solution)/shard_map/dynamic_update_slice | solution.py:206
  101.2 1.7 %fusion.14 = (bf16[32,32,4,256]{3,2,1,0:T(4,128)(2,1)S(1)}, bf16[32,32,4,256]{3,2,1,0:T(4,128)(2,1)S(1)}) fusion(bf16[32,32,24,256]{3,2,1,0:T(8,128)(2,1)S(1)} %constant_dynamic-update-slice_fusion), kind=kLoop, calls=%fused_computation.77 | loop fusion | bytes 8388608 | tf_op jit(solution)/shard_map/slice | solution.py:194
  103.5 1.3 collective-permute-start.7
  105.2 4.8 %collective-permute-start.5 = (bf16[3,8,8,4,256]{4,3,2,1,0:T(4,128)(2,1)S(1)}, bf16[3,8,8,4,256]{4,3,2,1,0:T(4,128)(2,1)S(1)}, u32[]{:S(2)}, u32[]{:S(2)}) collective-permute-start(bf16[3,8,8,4,256]{4,3,2,1,0:T(4,128)(2,1)S(1)} %pad_maximum_fusion.4), channel_id=1, source_target_pairs={{0,1},{2,3},{4,5},{6,7},{8,9},{10,11},{12,13},{14,15},{16,17},{18,... | collective-permute-start | bytes 1179656 | tf_op jit(solution)/shard_map/ppermute | solution.py:199
  110.2 6.5 %collective-permute-done.7 = bf16[3,8,8,4,256]{4,3,2,1,0:T(4,128)(2,1)S(1)} collective-permute-done((bf16[3,8,8,4,256]{4,3,2,1,0:T(4,128)(2,1)S(1)}, bf16[3,8,8,4,256]{4,3,2,1,0:T(4,128)(2,1)S(1)}, u32[]{:S(2)}, u32[]{:S(2)}) %collective-permute-start.7) | collective-permute-done | bytes 393248 | tf_op jit(solution)/shard_map/ppermute | solution.py:199
  116.8 1.5 %collective-permute-done.5 = bf16[3,8,8,4,256]{4,3,2,1,0:T(4,128)(2,1)S(1)} collective-permute-done((bf16[3,8,8,4,256]{4,3,2,1,0:T(4,128)(2,1)S(1)}, bf16[3,8,8,4,256]{4,3,2,1,0:T(4,128)(2,1)S(1)}, u32[]{:S(2)}, u32[]{:S(2)}) %collective-permute-start.5) | collective-permute-done | bytes 393248 | tf_op jit(solution)/shard_map/ppermute | solution.py:199
  120.8 8.1 %patches.1 = f32[4,64,320]{2,1,0:T(8,128)S(1)} custom-call(s32[4]{0:T(128)S(1)} %multiply_add_fusion.slot_ref, f32[30]{0:T(128)S(1)} %copy-done, bf16[2,3,256,4]{3,2,1,0:T(8,128)(2,1)S(1)} %pad_maximum_fusion.3.dofs_ref, bf16[4,512,256]{2,1,0:T(8,128)(2,1)S(1)} %pad_maximum_fusion.2.rows_ref), custom_call_target="tpu_custom_call" | custom-call | flops 1000000000 | bytes 2097152 | tf_op jit(solution)/shard_map/patches/pallas_call | solution.py:174
  128.9 9.4 %all_to_all.5 = f32[4,64,320]{2,1,0:T(8,128)S(1)} all-to-all(f32[4,64,320]{2,1,0:T(8,128)S(1)} %patches.1), channel_id=1, replica_groups=mesh['gx'=4,'gy'=4,'gz'=2] {'gz'}, dimensions={0} | all-to-all | bytes 655360 | tf_op jit(solution)/shard_map/all_to_all | solution.py:259
  (61 shorter events, 15.5 us)
Async XLA Ops:
  0.6 5.2 %copy-start.5 = (s32[4,512]{1,0:T(4,128)S(1)}, s32[4,512]{1,0:T(4,128)}, u32[]{:S(2)}) copy-start(s32[4,512]{1,0:T(4,128)} %param.11) | copy-start | bytes 24580
  3.4 48.9 %collective-permute-start = (bf16[4,24,24,256]{3,2,1,0:T(8,128)(2,1)}, bf16[4,24,24,256]{3,2,1,0:T(8,128)(2,1)S(1)}, u32[]{:S(2)}, u32[]{:S(2)}) collective-permute-start(bf16[4,24,24,256]{3,2,1,0:T(8,128)(2,1)} %get-tuple-element.17), channel_id=1, source_target_pairs={{0,8},{8,16},{16,24},{1,9},{9,17},{17,25},{2,10},{10,18},{18,26},{... | collective-permute-start | bytes 3538952 | tf_op jit(solution)/shard_map/ppermute | solution.py:199
  6.5 56.4 %collective-permute-start.4 = (s32[4]{0:T(128)}, s32[4]{0:T(128)}, u32[]{:S(2)}, u32[]{:S(2)}) collective-permute-start(s32[4]{0:T(128)} %slice_reduce_fusion.6), channel_id=1, source_target_pairs={{1,0},{3,2},{5,4},{7,6},{9,8},{11,10},{13,12},{15,14},{17,16},{19,... | collective-permute-start | bytes 56 | tf_op jit(solution)/shard_map/ppermute | solution.py:199
  7.8 64.3 %collective-permute-start.6 = (s32[4]{0:T(128)}, s32[4]{0:T(128)}, u32[]{:S(2)}, u32[]{:S(2)}) collective-permute-start(s32[4]{0:T(128)} %slice_reduce_fusion.6), channel_id=1, source_target_pairs={{0,1},{2,3},{4,5},{6,7},{8,9},{10,11},{12,13},{14,15},{16,17},{18,... | collective-permute-start | bytes 56 | tf_op jit(solution)/shard_map/ppermute | solution.py:199
  13.3 39.0 %collective-permute-start.1 = (bf16[4,24,24,256]{3,2,1,0:T(8,128)(2,1)S(1)}, bf16[4,24,24,256]{3,2,1,0:T(8,128)(2,1)S(1)}, u32[]{:S(2)}, u32[]{:S(2)}) collective-permute-start(bf16[4,24,24,256]{3,2,1,0:T(8,128)(2,1)S(1)} %get-tuple-element.16), channel_id=1, source_target_pairs={{8,0},{16,8},{24,16},{9,1},{17,9},{25,17},{10,2},{18,10},{26,18},{... | collective-permute-start | bytes 3538952 | tf_op jit(solution)/shard_map/ppermute | solution.py:199
  25.9 7.6 %copy-start.6 = (bf16[256]{0:T(256)(128)(2,1)S(1)}, bf16[256]{0:T(256)(128)(2,1)}, u32[]{:S(2)}) copy-start(bf16[256]{0:T(256)(128)(2,1)} %param.9) | copy-start | bytes 1540
  25.9 7.6 %copy-start.4 = (s32[4,512]{1,0:T(4,128)S(1)}, s32[4,512]{1,0:T(4,128)}, u32[]{:S(2)}) copy-start(s32[4,512]{1,0:T(4,128)} %param.10) | copy-start | bytes 24580
  53.7 38.6 %collective-permute-start.2 = (bf16[32,4,24,256]{3,2,1,0:T(8,128)(2,1)}, bf16[32,4,24,256]{3,2,1,0:T(8,128)(2,1)}, u32[]{:S(2)}, u32[]{:S(2)}) collective-permute-start(bf16[32,4,24,256]{3,2,1,0:T(8,128)(2,1)} %pad_maximum_fusion), channel_id=1, source_target_pairs={{0,2},{2,4},{4,6},{1,3},{3,5},{5,7},{8,10},{10,12},{12,14},{9,11},... | collective-permute-start | bytes 4718600 | tf_op jit(solution)/shard_map/ppermute | solution.py:199
  59.2 2.8 %copy-start.1 = (bf16[1,4,256]{2,1,0:T(4,128)(2,1)S(1)}, bf16[1,4,256]{2,1,0:T(4,128)(2,1)}, u32[]{:S(2)}) copy-start(bf16[1,4,256]{2,1,0:T(4,128)(2,1)} %squeeze.76) | copy-start | bytes 6148
  59.2 2.8 %copy-start.2 = (bf16[1,4,256]{2,1,0:T(4,128)(2,1)S(1)}, bf16[1,4,256]{2,1,0:T(4,128)(2,1)}, u32[]{:S(2)}) copy-start(bf16[1,4,256]{2,1,0:T(4,128)(2,1)} %squeeze.77) | copy-start | bytes 6148
  59.2 2.8 %copy-start.3 = (bf16[1,4,256]{2,1,0:T(4,128)(2,1)S(1)}, bf16[1,4,256]{2,1,0:T(4,128)(2,1)}, u32[]{:S(2)}) copy-start(bf16[1,4,256]{2,1,0:T(4,128)(2,1)} %squeeze.78) | copy-start | bytes 6148
  59.2 3.5 %copy-start.7 = (s32[4]{0:T(128)S(1)}, s32[4]{0:T(128)}, u32[]{:S(2)}) copy-start(s32[4]{0:T(128)} %param.14) | copy-start | bytes 52
  60.6 39.0 %collective-permute-start.3 = (bf16[32,4,24,256]{3,2,1,0:T(8,128)(2,1)}, bf16[32,4,24,256]{3,2,1,0:T(8,128)(2,1)}, u32[]{:S(2)}, u32[]{:S(2)}) collective-permute-start(bf16[32,4,24,256]{3,2,1,0:T(8,128)(2,1)} %pad_maximum_fusion.1), channel_id=1, source_target_pairs={{2,0},{4,2},{6,4},{3,1},{5,3},{7,5},{10,8},{12,10},{14,12},{11,9},... | collective-permute-start | bytes 4718600 | tf_op jit(solution)/shard_map/ppermute | solution.py:199
  103.5 13.2 %collective-permute-start.7 = (bf16[3,8,8,4,256]{4,3,2,1,0:T(4,128)(2,1)S(1)}, bf16[3,8,8,4,256]{4,3,2,1,0:T(4,128)(2,1)S(1)}, u32[]{:S(2)}, u32[]{:S(2)}) collective-permute-start(bf16[3,8,8,4,256]{4,3,2,1,0:T(4,128)(2,1)S(1)} %pad_maximum_fusion.5), channel_id=1, source_target_pairs={{1,0},{3,2},{5,4},{7,6},{9,8},{11,10},{13,12},{15,14},{17,16},{19,... | collective-permute-start | bytes 1179656 | tf_op jit(solution)/shard_map/ppermute | solution.py:199
  105.2 13.1 %collective-permute-start.5 = (bf16[3,8,8,4,256]{4,3,2,1,0:T(4,128)(2,1)S(1)}, bf16[3,8,8,4,256]{4,3,2,1,0:T(4,128)(2,1)S(1)}, u32[]{:S(2)}, u32[]{:S(2)}) collective-permute-start(bf16[3,8,8,4,256]{4,3,2,1,0:T(4,128)(2,1)S(1)} %pad_maximum_fusion.4), channel_id=1, source_target_pairs={{0,1},{2,3},{4,5},{6,7},{8,9},{10,11},{12,13},{14,15},{16,17},{18,... | collective-permute-start | bytes 1179656 | tf_op jit(solution)/shard_map/ppermute | solution.py:199
  120.1 0.7 copy-start

commit v3 on v2

--- a/solution.py
+++ b/solution.py
@@ -62,29 +62,35 @@
 
 
 def patch_kernel(slot_ref, omega_ref, dofs_ref, rows_ref, out_ref,
-                 red, black, bias_r, bias_k, gate_r, gate_k, root_r, root_k):
+                 red, black, bias_r, bias_k, gate_r, gate_k, root_r, root_k, load_r, load_k):
     patches = rows_ref.shape[0]
     lanes = patches * M
-    spot = jnp.where(
-        lax.broadcasted_iota(jnp.int32, (patches, lanes), 1) // M
-        == lax.broadcasted_iota(jnp.int32, (patches, lanes), 0), 1.0, 0.0).astype(jnp.bfloat16)
+    cells = dofs_ref[...].T.astype(jnp.bfloat16)
+    kinds = cells.shape[1]
+    owner = lax.broadcasted_iota(jnp.int32, (kinds, lanes), 1) // M
+    entry = lax.broadcasted_iota(jnp.int32, (kinds, lanes), 0)
     shape = (HALF, BOX, lanes)
     place = lax.broadcasted_iota(jnp.int32, shape, 1)
     column = lax.broadcasted_iota(jnp.int32, shape, 2) % M
     along = lax.broadcasted_iota(jnp.int32, shape, 0)
-    for color, (bias, gate, root) in enumerate(((bias_r, gate_r, root_r), (bias_k, gate_k, root_k))):
-        wide = [
-            jnp.dot(dofs_ref[color, kind], spot, preferred_element_type=jnp.float32).reshape(
-                (BOX, HALF, BOX, lanes))
-            for kind in range(3)
-        ]
-        for x in range(BOX):
-            live = wide[1][x]
-            scale = live * lax.rsqrt(wide[0][x])
-            member = (x // 2 * HALF + along) * HALF + place // 2 == column
+    wide = []
+    for kind in range(3):
+        spot = jnp.where(entry == kind * patches + owner, 1.0, 0.0).astype(jnp.bfloat16)
+        wide.append(jnp.dot(cells, spot, preferred_element_type=jnp.float32).reshape(
+            (BOX, HALF, 2, BOX, lanes)))
+    for x in range(BOX):
+        even = (place + x) % 2 == 0
+        member = (x // 2 * HALF + along) * HALF + place // 2 == column
+        pairs = [(w[x, :, 0], w[x, :, 1]) for w in wide]
+        for bias, gate, root, load, swap in (
+                (bias_r, gate_r, root_r, load_r, False), (bias_k, gate_k, root_k, load_k, True)):
+            coef, live, weight = [
+                jnp.where(even, b, a) if swap else jnp.where(even, a, b) for a, b in pairs]
+            scale = live * lax.rsqrt(coef)
             root[x] = scale
             gate[x] = live * (1.0 / diag_shift)
-            bias[x] = jnp.where(member, scale * wide[2][x] * (1.0 / diag_shift), 0.0)
+            load[x] = scale * weight
+            bias[x] = jnp.where(member, scale * weight * (1.0 / diag_shift), 0.0)
     red[...] = bias_r[...]
     black[...] = jnp.zeros(black.shape, jnp.float32)
     relax(black, red, bias_k, gate_k, omega_ref[1], 1, place)
@@ -98,8 +104,8 @@
     for x2 in range(BOX // 2):
         solved, size = 0.0, 0.0
         for x in (2 * x2, 2 * x2 + 1):
-            for color, (grid, bias, root) in enumerate(((red, bias_r, root_r), (black, bias_k, root_k))):
-                solved = solved + reduce_weight(dofs_ref, spot, color, x, lanes) * root[x] * grid[x]
+            for grid, bias, load in ((red, bias_r, load_r), (black, bias_k, load_k)):
+                solved = solved + load[x] * grid[x]
                 size = size + bias[x] * bias[x]
             first = red[x] * root_r[x]
             second = black[x] * root_k[x]
@@ -149,22 +155,9 @@
         out_ref[slot_ref[p], :, :width] = exact_dot(block, projected)
 
 
-def reduce_weight(dofs_ref, spot, color, x, lanes):
-    block = dofs_ref[color, 2, x * HALF * BOX:(x + 1) * HALF * BOX]
-    return jnp.dot(block, spot, preferred_element_type=jnp.float32).reshape((HALF, BOX, lanes))
-
-
-def two_colors(values):
-    patches = values.shape[0]
-    cells = values.reshape(patches, BOX, HALF, 2, BOX)
-    odd = (jnp.arange(BOX)[:, None, None] + jnp.arange(BOX)[None, None, :]) % 2
-    first, second = cells[:, :, :, 0], cells[:, :, :, 1]
-    both = jnp.stack([jnp.where(odd == 0, first, second), jnp.where(odd == 0, second, first)])
-    return both.reshape(2, patches, PATCH // 2).transpose(0, 2, 1)
-
-
 def coarse_parts(target_slot, slot_count, coefficient, live, weights, patch_rows):
-    dofs = jnp.stack([two_colors(v.astype(jnp.bfloat16)) for v in (coefficient, live, weights)], axis=1)
+    dofs = jnp.concatenate([v.astype(jnp.float32) for v in (coefficient, live, weights)], axis=0)
+    dofs = jnp.pad(dofs, ((0, -dofs.shape[0] % 16), (0, 0)))
     patches = patch_rows.shape[0]
     lanes = patches * M
     omega = jnp.array(relaxation(), jnp.float32)
@@ -176,7 +169,7 @@
         out_shape=jax.ShapeDtypeStruct((slot_count, M, patch_rows.shape[-1] + M), jnp.float32),
         in_specs=[smem, smem, vmem, vmem],
         out_specs=vmem,
-        scratch_shapes=[grid] * 8,
+        scratch_shapes=[grid] * 10,
         compiler_params=pltpu.CompilerParams(vmem_limit_bytes=40 * 1024 * 1024),
         cost_estimate=pl.CostEstimate(flops=10**9, bytes_accessed=2**21, transcendentals=0),
         name="patches",
@@ -208,7 +201,11 @@
 
 def boxes(fine_rhs, localization):
     extent = [n + 2 * HW for n in fine_rhs.shape[:3]]
-    corner = localization[:, 0]
+    first = localization[:, 0]
+    corner = jnp.stack([
+        lax.div(first, extent[1] * extent[2]),
+        lax.rem(lax.div(first, extent[2]), extent[1]),
+        lax.rem(first, extent[2])])
     lower, upper = exchanged(corner, corner, "gz")
     before, after = exchanged(*edges(fine_rhs, 0), "gx")
     y_last, y_first = edges(fine_rhs, 1)
@@ -217,24 +214,29 @@
     y_before, y_after = exchanged(last_y, first_y, "gy")
     wide = widened(widened(fine_rhs, before, after, 0), y_before, y_after, 1)
 
-    def window(source, first):
-        at = (first // (extent[1] * extent[2]), first // extent[2] % extent[1], 0, 0)
-        return lax.dynamic_slice(source, at, (BOX, BOX) + source.shape[2:])
+    zero = jnp.int32(0)
+
+    def window(source, at, p):
+        return lax.dynamic_slice(
+            source, (at[0, p], at[1, p], zero, zero), (BOX, BOX) + source.shape[2:],
+            allow_negative_indices=False)
 
     count = localization.shape[0]
     rising = [p for p in range(count) if p != 1]
     falling = [p for p in range(count) if p != 0]
     z_last, z_first = edges(wide, 2)
-    sent_up = jnp.stack([window(z_last, upper[p]) for p in rising])
-    sent_down = jnp.stack([window(z_first, lower[p]) for p in falling])
+    sent_up = jnp.stack([window(z_last, upper, p) for p in rising])
+    sent_down = jnp.stack([window(z_first, lower, p) for p in falling])
     z_before, z_after = exchanged(sent_up, sent_down, "gz")
     nothing = jnp.zeros((BOX, BOX, HW, fine_rhs.shape[-1]), fine_rhs.dtype)
     rows = []
     for p in range(count):
         low = z_before[rising.index(p)] if p in rising else nothing
         top = z_after[falling.index(p)] if p in falling else nothing
-        column = jnp.concatenate([low, window(wide, corner[p]), top], axis=2)
-        box = lax.dynamic_slice_in_dim(column, corner[p] % extent[2], BOX, axis=2)
+        column = jnp.concatenate([low, window(wide, corner, p), top], axis=2)
+        box = lax.dynamic_slice(
+            column, (zero, zero, corner[2, p], zero), (BOX, BOX, BOX, column.shape[3]),
+            allow_negative_indices=False)
         rows.append(box.reshape(PATCH, -1))
     return jnp.stack(rows)
 

time: 141 us -> 106 us (0.75)
  the two profiles are of different devices: /device:TPU:0 before, /device:TPU:1 now
where the time goes in v3:
time: 106 us; the launch traced here: 104 us
  local copies, waits for them, and re-layouts  43.2 us (41%)
  starting transfers between devices  22.8 us (22%)
  waiting for transfers between devices  13.4 us (13%)
  other arithmetic  8.5 us (8%)
  Pallas kernels  8.42 us (8%)
  blocking collectives  7.13 us (7%)
    ppermute x8, starting transfers between devices, exchanged(): return (lax.ppermute(last, axis, up), lax.ppermute(first, axis, down))  22.8 us
    ppermute x8, waiting for transfers between devices, exchanged(): return (lax.ppermute(last, axis, up), lax.ppermute(first, axis, down))  13.4 us
    pad x2, local copies, waits for them, and re-layouts, widened(): wide = lax.pad(array, jnp.zeros((), array.dtype), pad)  13.3 us
    pallas_call x1, Pallas kernels, coarse_parts(): pl.pallas_call(patch_kernel, out_shape=jax.ShapeDtypeStruct((slot_count,...  8.42 us
    another operation x1, local copies, waits for them, and re-layouts, boxes(): sent_down = jnp.stack([window(z_first, lower, p) for p in falling])  7.89 us
    all_to_all x1, blocking collectives, local(): lax.all_to_all(results, 'gz', split_axis=0, concat_axis=0, tiled=True)  7.13 us
    dynamic_slice x1, local copies, waits for them, and re-layouts, window(): lax.dynamic_slice(source, (at[0, p], at[1, p], zero, zero), (BOX, BOX) +...  5.31 us
    slice x5, local copies, waits for them, and re-layouts, edges(): lax.slice_in_dim(array, 0, HW, axis=dim)  5.29 us
  transfers between devices with their start and end apart: 8, of which 2 were waited for; matrix products, arithmetic and copies ran while one was open for 29% of the time, Pallas kernels for 0%

profile of v3, /device:TPU:1, one launch (start us, length us, event | category | flops | bytes accessed | tf_op | source)
XLA Modules:
  0.0 104.4 jit_solution(6838653622299190943)
XLA Ops:
  0.6 1.8 %fusion.12 = (bf16[4,24,24,256]{3,2,1,0:T(8,128)(2,1)S(1)}, bf16[4,24,24,256]{3,2,1,0:T(8,128)(2,1)S(1)}) fusion(bf16[24,24,24,256]{3,2,1,0:T(8,128)(2,1)} %param.8), kind=kLoop, calls=%fused_computation.67 | loop fusion | bytes 4718592 | tf_op jit(solution)/shard_map/slice | solution.py:187
  2.4 4.5 %collective-permute-start = (bf16[4,24,24,256]{3,2,1,0:T(8,128)(2,1)S(1)}, bf16[4,24,24,256]{3,2,1,0:T(8,128)(2,1)S(1)}, u32[]{:S(2)}, u32[]{:S(2)}) collective-permute-start(bf16[4,24,24,256]{3,2,1,0:T(8,128)(2,1)S(1)} %get-tuple-element.11), channel_id=1, source_target_pairs={{0,8},{8,16},{16,24},{1,9},{9,17},{17,25},{2,10},{10,18},{18,26},{... | collective-permute-start | bytes 3538952 | tf_op jit(solution)/shard_map/ppermute | solution.py:192
  6.9 1.9 %collective-permute-start.1 = (bf16[4,24,24,256]{3,2,1,0:T(8,128)(2,1)S(1)}, bf16[4,24,24,256]{3,2,1,0:T(8,128)(2,1)S(1)}, u32[]{:S(2)}, u32[]{:S(2)}) collective-permute-start(bf16[4,24,24,256]{3,2,1,0:T(8,128)(2,1)S(1)} %get-tuple-element.10), channel_id=1, source_target_pairs={{8,0},{16,8},{24,16},{9,1},{17,9},{25,17},{10,2},{18,10},{26,18},{... | collective-permute-start | bytes 3538952 | tf_op jit(solution)/shard_map/ppermute | solution.py:192
  8.9 0.8 slice_reduce_fusion
  9.7 1.8 %fusion.11 = (bf16[24,4,24,256]{3,2,1,0:T(8,128)(2,1)S(1)}, bf16[24,4,24,256]{3,2,1,0:T(8,128)(2,1)S(1)}) fusion(bf16[24,24,24,256]{3,2,1,0:T(8,128)(2,1)} %param.8), kind=kLoop, calls=%fused_computation.66 | loop fusion | bytes 4718592 | tf_op jit(solution)/shard_map/slice | solution.py:187
  11.4 8.6 %collective-permute-done = bf16[4,24,24,256]{3,2,1,0:T(8,128)(2,1)S(1)} collective-permute-done((bf16[4,24,24,256]{3,2,1,0:T(8,128)(2,1)S(1)}, bf16[4,24,24,256]{3,2,1,0:T(8,128)(2,1)S(1)}, u32[]{:S(2)}, u32[]{:S(2)}) %collective-permute-start) | collective-permute-done | bytes 1179680 | tf_op jit(solution)/shard_map/ppermute | solution.py:192
  20.1 4.8 %collective-permute-done.1 = bf16[4,24,24,256]{3,2,1,0:T(8,128)(2,1)S(1)} collective-permute-done((bf16[4,24,24,256]{3,2,1,0:T(8,128)(2,1)S(1)}, bf16[4,24,24,256]{3,2,1,0:T(8,128)(2,1)S(1)}, u32[]{:S(2)}, u32[]{:S(2)}) %collective-permute-start.1) | collective-permute-done | bytes 1179680 | tf_op jit(solution)/shard_map/ppermute | solution.py:192
  24.9 1.3 %pad_maximum_fusion = bf16[32,4,24,256]{3,2,1,0:T(8,128)(2,1)} fusion(bf16[4,4,24,256]{3,2,1,0:T(8,128)(2,1)S(1)} %get-tuple-element.21, bf16[24,4,24,256]{3,2,1,0:T(8,128)(2,1)S(1)} %get-tuple-element.9, bf16[4,4,24,256]{3,2,1,0:T(8,128)(2,1)S(1)} %get-tuple-element.19), kind=kLoop, calls=%fused_computation.2 | loop fusion | flops 1572864 | bytes 3145728 | tf_op jit(solution)/shard_map/concatenate | solution.py:212
  26.2 4.4 %collective-permute-start.2 = (bf16[32,4,24,256]{3,2,1,0:T(8,128)(2,1)}, bf16[32,4,24,256]{3,2,1,0:T(8,128)(2,1)}, u32[]{:S(2)}, u32[]{:S(2)}) collective-permute-start(bf16[32,4,24,256]{3,2,1,0:T(8,128)(2,1)} %pad_maximum_fusion), channel_id=1, source_target_pairs={{0,2},{2,4},{4,6},{1,3},{3,5},{5,7},{8,10},{10,12},{12,14},{9,11},... | collective-permute-start | bytes 4718600 | tf_op jit(solution)/shard_map/ppermute | solution.py:192
  30.6 1.4 %pad_maximum_fusion.1 = bf16[32,4,24,256]{3,2,1,0:T(8,128)(2,1)} fusion(bf16[4,4,24,256]{3,2,1,0:T(8,128)(2,1)S(1)} %get-tuple-element.20, bf16[24,4,24,256]{3,2,1,0:T(8,128)(2,1)S(1)} %get-tuple-element.8, bf16[4,4,24,256]{3,2,1,0:T(8,128)(2,1)S(1)} %get-tuple-element.18), kind=kLoop, calls=%fused_computation.3 | loop fusion | flops 1572864 | bytes 3145728 | tf_op jit(solution)/shard_map/concatenate | solution.py:213
  32.0 1.3 %collective-permute-start.3 = (bf16[32,4,24,256]{3,2,1,0:T(8,128)(2,1)}, bf16[32,4,24,256]{3,2,1,0:T(8,128)(2,1)}, u32[]{:S(2)}, u32[]{:S(2)}) collective-permute-start(bf16[32,4,24,256]{3,2,1,0:T(8,128)(2,1)} %pad_maximum_fusion.1), channel_id=1, source_target_pairs={{2,0},{4,2},{6,4},{3,1},{5,3},{7,5},{10,8},{12,10},{14,12},{11,9},... | collective-permute-start | bytes 4718600 | tf_op jit(solution)/shard_map/ppermute | solution.py:192
  33.3 1.4 %collective-permute-start.4 = (s32[3,4]{1,0:T(4,128)S(1)}, s32[3,4]{1,0:T(4,128)S(1)}, u32[]{:S(2)}, u32[]{:S(2)}) collective-permute-start(s32[3,4]{1,0:T(4,128)S(1)} %pad_add_fusion), channel_id=1, source_target_pairs={{1,0},{3,2},{5,4},{7,6},{9,8},{11,10},{13,12},{15,14},{17,16},{19,... | collective-permute-start | bytes 152 | tf_op jit(solution)/shard_map/ppermute | solution.py:192
  34.8 4.0 %collective-permute-start.6 = (s32[3,4]{1,0:T(4,128)S(1)}, s32[3,4]{1,0:T(4,128)S(1)}, u32[]{:S(2)}, u32[]{:S(2)}) collective-permute-start(s32[3,4]{1,0:T(4,128)S(1)} %pad_add_fusion), channel_id=1, source_target_pairs={{0,1},{2,3},{4,5},{6,7},{8,9},{10,11},{12,13},{14,15},{16,17},{18,... | collective-permute-start | bytes 152 | tf_op jit(solution)/shard_map/ppermute | solution.py:192
  38.8 7.6 %pad.11 = bf16[32,24,24,256]{3,2,1,0:T(8,128)(2,1)} pad(bf16[24,24,24,256]{3,2,1,0:T(8,128)(2,1)} %param.8, bf16[]{:T(256)} %constant.24.clone.1), padding=4_4x0_0x0_0x0_0 | pad | bytes 16515074 | tf_op jit(solution)/shard_map/pad | solution.py:197
  47.1 0.8 select_reduce_fusion
  49.4 1.1 %constant_dynamic-update-slice_fusion.3 = bf16[32,24,24,256]{3,2,1,0:T(8,128)(2,1)} fusion(bf16[32,24,24,256]{3,2,1,0:T(8,128)(2,1)} %pad.11, bf16[4,24,24,256]{3,2,1,0:T(8,128)(2,1)S(1)} %collective-permute-done), kind=kLoop, calls=%fused_computation.50 | loop fusion | bytes 2359296 | tf_op jit(solution)/shard_map/dynamic_update_slice | solution.py:198
  50.6 1.2 %constant_dynamic-update-slice_fusion.2 = bf16[32,24,24,256]{3,2,1,0:T(8,128)(2,1)} fusion(bf16[32,24,24,256]{3,2,1,0:T(8,128)(2,1)} %constant_dynamic-update-slice_fusion.3, bf16[4,24,24,256]{3,2,1,0:T(8,128)(2,1)S(1)} %collective-permute-done.1), kind=kLoop, calls=%fused_computation.49 | loop fusion | bytes 2359296 | tf_op jit(solution)/shard_map/dynamic_update_slice | solution.py:199
  51.8 5.7 %pad.12 = bf16[32,32,24,256]{3,2,1,0:T(8,128)(2,1)S(1)} pad(bf16[32,24,24,256]{3,2,1,0:T(8,128)(2,1)} %constant_dynamic-update-slice_fusion.2, bf16[]{:T(256)} %constant.24.clone.1), padding=0_0x4_4x0_0x0_0 | pad | bytes 22020098 | tf_op jit(solution)/shard_map/pad | solution.py:197
  57.5 1.5 %constant_dynamic-update-slice_fusion.1 = bf16[32,32,24,256]{3,2,1,0:T(8,128)(2,1)S(1)} fusion(bf16[32,32,24,256]{3,2,1,0:T(8,128)(2,1)S(1)} %pad.12, bf16[32,4,24,256]{3,2,1,0:T(8,128)(2,1)} %collective-permute-done.2), kind=kLoop, calls=%fused_computation.48 | loop fusion | bytes 3145728 | tf_op jit(solution)/shard_map/dynamic_update_slice | solution.py:198
  59.1 1.5 %constant_dynamic-update-slice_fusion = bf16[32,32,24,256]{3,2,1,0:T(8,128)(2,1)S(1)} fusion(bf16[32,32,24,256]{3,2,1,0:T(8,128)(2,1)S(1)} %constant_dynamic-update-slice_fusion.1, bf16[32,4,24,256]{3,2,1,0:T(8,128)(2,1)} %collective-permute-done.3), kind=kLoop, calls=%fused_computation.47 | loop fusion | bytes 3145728 | tf_op jit(solution)/shard_map/dynamic_update_slice | solution.py:199
  60.6 1.7 %fusion.10 = (bf16[32,32,4,256]{3,2,1,0:T(4,128)(2,1)S(1)}, bf16[32,32,4,256]{3,2,1,0:T(4,128)(2,1)S(1)}) fusion(bf16[32,32,24,256]{3,2,1,0:T(8,128)(2,1)S(1)} %constant_dynamic-update-slice_fusion), kind=kLoop, calls=%fused_computation.65 | loop fusion | bytes 8388608 | tf_op jit(solution)/shard_map/slice | solution.py:187
  62.3 7.9 %dynamic-slice_bitcast_fusion.2 = (bf16[1,8,8,4,256]{4,3,2,1,0:T(4,128)(2,1)S(1)}, bf16[1,8,8,4,256]{4,3,2,1,0:T(4,128)(2,1)S(1)}, bf16[1,8,8,4,256]{4,3,2,1,0:T...) fusion(bf16[32,32,4,256]{3,2,1,0:T(4,128)(2,1)S(1)} %get-tuple-, ...), kind=kLoop, calls=%fused_computation.36 | loop fusion | bytes 1572912 | tf_op jit(solution)/shard_map/stack | solution.py:229
  70.5 1.3 %collective-permute-start.7 = (bf16[3,8,8,4,256]{4,3,2,1,0:T(4,128)(2,1)S(1)}, bf16[3,8,8,4,256]{4,3,2,1,0:T(4,128)(2,1)S(1)}, u32[]{:S(2)}, u32[]{:S(2)}) collective-permute-start(bf16[3,8,8,4,256]{4,3,2,1,0:T(4,128)(2,1)S(1)} %pad_maximum_fusion.4), channel_id=1, source_target_pairs={{1,0},{3,2},{5,4},{7,6},{9,8},{11,10},{13,12},{15,14},{17,16},{19,... | collective-permute-start | bytes 1179656 | tf_op jit(solution)/shard_map/ppermute | solution.py:192
  72.7 4.0 %collective-permute-start.5 = (bf16[3,8,8,4,256]{4,3,2,1,0:T(4,128)(2,1)S(1)}, bf16[3,8,8,4,256]{4,3,2,1,0:T(4,128)(2,1)S(1)}, u32[]{:S(2)}, u32[]{:S(2)}) collective-permute-start(bf16[3,8,8,4,256]{4,3,2,1,0:T(4,128)(2,1)S(1)} %pad_maximum_fusion.3), channel_id=1, source_target_pairs={{0,1},{2,3},{4,5},{6,7},{8,9},{10,11},{12,13},{14,15},{16,17},{18,... | collective-permute-start | bytes 1179656 | tf_op jit(solution)/shard_map/ppermute | solution.py:192
  76.8 5.3 %constant_dynamic-slice_fusion.3 = (bf16[8,8,24,256]{3,2,1,0:T(8,128)(2,1)S(1)}, bf16[8,8,24,256]{3,2,1,0:T(8,128)(2,1)S(1)}, bf16[8,8,24,256]{3,2,1,0:T(8,128)(2,1)S(1)}, bf16[8,8,24,256]{3,2,1,0:T(8,128)(2,1)S(1)}) fusion(bf16[32,32,24,256]{3,2,1,0:T(8,128)(2,1)S(1)} %constant_dynamic-update-slice_fusion, s32[]{:T(128)} %bitcast.10, s32[]{:T(128)} %bitcast.11, ...), kind=kLoop, calls=%fused_computation.46 | loop fusion | bytes 6291488 | tf_op jit(solution)/shard_map/dynamic_slice | solution.py:220
  82.4 0.9 fusion.6
  83.4 1.0 fusion.4
  84.4 2.1 %fusion.1 = (bf16[8,8,8,256]{3,2,1,0:T(8,128)(2,1)S(1)}, bf16[8,8,8,256]{3,2,1,0:T(8,128)(2,1)S(1)}) fusion(s32[]{:T(128)} %bitcast.12, bf16[8,8,4,256]{3,2,1,0:T(4,128)(2,1)S(1)} %broadcast_in_dim.34, bf16[8,8,4,256]{3,2,1,0:T(4,128)(2,1)S(1)} %get-tuple-element.22, bf16[8,8,24,256]{3,2,1,0:T(8,128)(2,1)S(1)} %get-tuple-element.2, s32[]{:T(128)} %bitcast.26, ...), kind=kLoop, calls=%fused_computation.20 | loop fusion | flops 1572864 | bytes 2490376 | tf_op jit(solution)/shard_map/concatenate | solution.py:236
  87.2 8.4 %patches.1 = f32[4,64,320]{2,1,0:T(8,128)S(1)} custom-call(s32[4]{0:T(128)S(1)} %multiply_add_fusion.slot_ref, f32[30]{0:T(128)S(1)} %copy-done, f32[16,512]{1,0:T(8,128)S(1)} %select_maximum_fusion.dofs_ref, bf16[4,512,256]{2,1,0:T(8,128)(2,1)S(1)} %pad_maximum_fusion.2.rows_ref), custom_call_target="tpu_custom_call" | custom-call | flops 1000000000 | bytes 2097152 | tf_op jit(solution)/shard_map/patches/pallas_call | solution.py:167
  95.6 7.1 %all_to_all.5 = f32[4,64,320]{2,1,0:T(8,128)S(1)} all-to-all(f32[4,64,320]{2,1,0:T(8,128)S(1)} %patches.1), channel_id=1, replica_groups=mesh['gx'=4,'gy'=4,'gz'=2] {'gz'}, dimensions={0} | all-to-all | bytes 655360 | tf_op jit(solution)/shard_map/all_to_all | solution.py:261
  102.7 0.9 copy.10
  103.6 0.7 reshape.107
  (40 shorter events, 4.6 us)
Async XLA Ops:
  2.4 17.6 %collective-permute-start = (bf16[4,24,24,256]{3,2,1,0:T(8,128)(2,1)S(1)}, bf16[4,24,24,256]{3,2,1,0:T(8,128)(2,1)S(1)}, u32[]{:S(2)}, u32[]{:S(2)}) collective-permute-start(bf16[4,24,24,256]{3,2,1,0:T(8,128)(2,1)S(1)} %get-tuple-element.11), channel_id=1, source_target_pairs={{0,8},{8,16},{16,24},{1,9},{9,17},{17,25},{2,10},{10,18},{18,26},{... | collective-permute-start | bytes 3538952 | tf_op jit(solution)/shard_map/ppermute | solution.py:192
  6.9 17.9 %collective-permute-start.1 = (bf16[4,24,24,256]{3,2,1,0:T(8,128)(2,1)S(1)}, bf16[4,24,24,256]{3,2,1,0:T(8,128)(2,1)S(1)}, u32[]{:S(2)}, u32[]{:S(2)}) collective-permute-start(bf16[4,24,24,256]{3,2,1,0:T(8,128)(2,1)S(1)} %get-tuple-element.10), channel_id=1, source_target_pairs={{8,0},{16,8},{24,16},{9,1},{17,9},{25,17},{10,2},{18,10},{26,18},{... | collective-permute-start | bytes 3538952 | tf_op jit(solution)/shard_map/ppermute | solution.py:192
  26.2 31.3 %collective-permute-start.2 = (bf16[32,4,24,256]{3,2,1,0:T(8,128)(2,1)}, bf16[32,4,24,256]{3,2,1,0:T(8,128)(2,1)}, u32[]{:S(2)}, u32[]{:S(2)}) collective-permute-start(bf16[32,4,24,256]{3,2,1,0:T(8,128)(2,1)} %pad_maximum_fusion), channel_id=1, source_target_pairs={{0,2},{2,4},{4,6},{1,3},{3,5},{5,7},{8,10},{10,12},{12,14},{9,11},... | collective-permute-start | bytes 4718600 | tf_op jit(solution)/shard_map/ppermute | solution.py:192
  32.0 27.1 %collective-permute-start.3 = (bf16[32,4,24,256]{3,2,1,0:T(8,128)(2,1)}, bf16[32,4,24,256]{3,2,1,0:T(8,128)(2,1)}, u32[]{:S(2)}, u32[]{:S(2)}) collective-permute-start(bf16[32,4,24,256]{3,2,1,0:T(8,128)(2,1)} %pad_maximum_fusion.1), channel_id=1, source_target_pairs={{2,0},{4,2},{6,4},{3,1},{5,3},{7,5},{10,8},{12,10},{14,12},{11,9},... | collective-permute-start | bytes 4718600 | tf_op jit(solution)/shard_map/ppermute | solution.py:192
  33.3 13.1 %copy-start.4 = (bf16[256]{0:T(256)(128)(2,1)S(1)}, bf16[256]{0:T(256)(128)(2,1)}, u32[]{:S(2)}) copy-start(bf16[256]{0:T(256)(128)(2,1)} %param.9) | copy-start | bytes 1540
  33.3 13.1 %copy-start.1 = (s32[4,512]{1,0:T(4,128)S(1)}, s32[4,512]{1,0:T(4,128)}, u32[]{:S(2)}) copy-start(s32[4,512]{1,0:T(4,128)} %param.12) | copy-start | bytes 24580
  33.3 13.1 %copy-start.3 = (bf16[4,512]{1,0:T(4,128)(2,1)S(1)}, bf16[4,512]{1,0:T(4,128)(2,1)}, u32[]{:S(2)}) copy-start(bf16[4,512]{1,0:T(4,128)(2,1)} %param.13) | copy-start | bytes 12292
  33.3 13.8 %copy-start.2 = (s32[4,512]{1,0:T(4,128)S(1)}, s32[4,512]{1,0:T(4,128)}, u32[]{:S(2)}) copy-start(s32[4,512]{1,0:T(4,128)} %param.10) | copy-start | bytes 24580
  33.3 14.6 %copy-start.5 = (s32[4]{0:T(128)S(1)}, s32[4]{0:T(128)}, u32[]{:S(2)}) copy-start(s32[4]{0:T(128)} %param.14) | copy-start | bytes 52
  33.3 14.8 %collective-permute-start.4 = (s32[3,4]{1,0:T(4,128)S(1)}, s32[3,4]{1,0:T(4,128)S(1)}, u32[]{:S(2)}, u32[]{:S(2)}) collective-permute-start(s32[3,4]{1,0:T(4,128)S(1)} %pad_add_fusion), channel_id=1, source_target_pairs={{1,0},{3,2},{5,4},{7,6},{9,8},{11,10},{13,12},{15,14},{17,16},{19,... | collective-permute-start | bytes 152 | tf_op jit(solution)/shard_map/ppermute | solution.py:192
  34.8 14.0 %collective-permute-start.6 = (s32[3,4]{1,0:T(4,128)S(1)}, s32[3,4]{1,0:T(4,128)S(1)}, u32[]{:S(2)}, u32[]{:S(2)}) collective-permute-start(s32[3,4]{1,0:T(4,128)S(1)} %pad_add_fusion), channel_id=1, source_target_pairs={{0,1},{2,3},{4,5},{6,7},{8,9},{10,11},{12,13},{14,15},{16,17},{18,... | collective-permute-start | bytes 152 | tf_op jit(solution)/shard_map/ppermute | solution.py:192
  70.5 11.6 %collective-permute-start.7 = (bf16[3,8,8,4,256]{4,3,2,1,0:T(4,128)(2,1)S(1)}, bf16[3,8,8,4,256]{4,3,2,1,0:T(4,128)(2,1)S(1)}, u32[]{:S(2)}, u32[]{:S(2)}) collective-permute-start(bf16[3,8,8,4,256]{4,3,2,1,0:T(4,128)(2,1)S(1)} %pad_maximum_fusion.4), channel_id=1, source_target_pairs={{1,0},{3,2},{5,4},{7,6},{9,8},{11,10},{13,12},{15,14},{17,16},{19,... | collective-permute-start | bytes 1179656 | tf_op jit(solution)/shard_map/ppermute | solution.py:192
  72.7 9.5 %collective-permute-start.5 = (bf16[3,8,8,4,256]{4,3,2,1,0:T(4,128)(2,1)S(1)}, bf16[3,8,8,4,256]{4,3,2,1,0:T(4,128)(2,1)S(1)}, u32[]{:S(2)}, u32[]{:S(2)}) collective-permute-start(bf16[3,8,8,4,256]{4,3,2,1,0:T(4,128)(2,1)S(1)} %pad_maximum_fusion.3), channel_id=1, source_target_pairs={{0,1},{2,3},{4,5},{6,7},{8,9},{10,11},{12,13},{14,15},{16,17},{18,... | collective-permute-start | bytes 1179656 | tf_op jit(solution)/shard_map/ppermute | solution.py:192
  86.5 0.7 copy-start

commit v4 on v3

--- a/solution.py
+++ b/solution.py
@@ -192,13 +192,6 @@
     return lax.ppermute(last, axis, up), lax.ppermute(first, axis, down)
 
 
-def widened(array, before, after, dim):
-    pad = [(HW, HW, 0) if d == dim else (0, 0, 0) for d in range(array.ndim)]
-    wide = lax.pad(array, jnp.zeros((), array.dtype), pad)
-    wide = lax.dynamic_update_slice_in_dim(wide, before, 0, axis=dim)
-    return lax.dynamic_update_slice_in_dim(wide, after, array.shape[dim] + HW, axis=dim)
-
-
 def boxes(fine_rhs, localization):
     extent = [n + 2 * HW for n in fine_rhs.shape[:3]]
     first = localization[:, 0]
@@ -212,7 +205,11 @@
     last_y = jnp.concatenate([edges(before, 1)[0], y_last, edges(after, 1)[0]], axis=0)
     first_y = jnp.concatenate([edges(before, 1)[1], y_first, edges(after, 1)[1]], axis=0)
     y_before, y_after = exchanged(last_y, first_y, "gy")
-    wide = widened(widened(fine_rhs, before, after, 0), y_before, y_after, 1)
+    side, none = (HW, HW, 0), (0, 0, 0)
+    wide = lax.pad(fine_rhs, jnp.zeros((), fine_rhs.dtype), [side, side, none, none])
+    for piece, at in ((before, (0, HW)), (after, (extent[0] - HW, HW)),
+                      (y_before, (0, 0)), (y_after, (0, extent[1] - HW))):
+        wide = lax.dynamic_update_slice(wide, piece, at + (0, 0))
 
     zero = jnp.int32(0)
 

time: 106 us -> 99.8 us (0.942)
  local copies, waits for them, and re-layouts: 43.2 us -> 27.6 us
  waiting for transfers between devices: 13.4 us -> 28.2 us
  starting transfers between devices: 22.8 us -> 20 us
  other arithmetic: 8.5 us -> 6.2 us
    ppermute x8, waiting for transfers between devices: 13.4 us -> 28.2 us  [exchanged(): return (lax.ppermute(last, axis, up), lax.ppermute(first, axis, down))]
    pad x2 -> x1, local copies, waits for them, and re-layouts: 13.3 us -> 2.46 us  [boxes(): lax.pad(fine_rhs, jnp.zeros((), fine_rhs.dtype), [side, side, none, none])]
    dynamic_update_slice x4, local copies, waits for them, and re-layouts: 5.39 us -> 0.39 us  [boxes(): wide = lax.dynamic_update_slice(wide, piece, at + (0, 0))]
    ppermute x8, starting transfers between devices: 22.8 us -> 20 us  [exchanged(): return (lax.ppermute(last, axis, up), lax.ppermute(first, axis, down))]
    concatenate x1, other arithmetic: 1.37 us -> 0.19 us  [boxes(): jnp.concatenate([edges(before, 1)[1], y_first, edges(after, 1)[1]], axis=0)]
    concatenate x1, other arithmetic: 1.32 us -> 0.19 us  [boxes(): jnp.concatenate([edges(before, 1)[0], y_last, edges(after, 1)[0]], axis=0)]
  transfers between devices with their start and end apart: 8 -> 8, of which waited for: 2 -> 5; matrix products, arithmetic and copies ran while one was open for 29% -> 15% of each run, Pallas kernels for 0% -> 0%
where the time goes in v4:
time: 99.8 us; the launch traced here: 98.7 us
  waiting for transfers between devices  28.2 us (28%)
  local copies, waits for them, and re-layouts  27.6 us (28%)
  starting transfers between devices  20 us (20%)
  Pallas kernels  8.42 us (8%)
  blocking collectives  7.13 us (7%)
  other arithmetic  6.2 us (6%)
  between operations  1.03 us (1%)
    ppermute x8, waiting for transfers between devices, exchanged(): return (lax.ppermute(last, axis, up), lax.ppermute(first, axis, down))  28.2 us
    ppermute x8, starting transfers between devices, exchanged(): return (lax.ppermute(last, axis, up), lax.ppermute(first, axis, down))  20 us
    pallas_call x1, Pallas kernels, coarse_parts(): pl.pallas_call(patch_kernel, out_shape=jax.ShapeDtypeStruct((slot_count,...  8.42 us
    another operation x1, local copies, waits for them, and re-layouts, boxes(): sent_down = jnp.stack([window(z_first, lower, p) for p in falling])  7.81 us
    all_to_all x1, blocking collectives, local(): lax.all_to_all(results, 'gz', split_axis=0, concat_axis=0, tiled=True)  7.13 us
    slice x5, local copies, waits for them, and re-layouts, edges(): lax.slice_in_dim(array, 0, HW, axis=dim)  5.59 us
    dynamic_slice x1, local copies, waits for them, and re-layouts, window(): lax.dynamic_slice(source, (at[0, p], at[1, p], zero, zero), (BOX, BOX) +...  5.41 us
    concatenate x3, other arithmetic, boxes(): column = jnp.concatenate([low, window(wide, corner, p), top], axis=2)  4.02 us
  transfers between devices with their start and end apart: 8, of which 5 were waited for; matrix products, arithmetic and copies ran while one was open for 15% of the time, Pallas kernels for 0%

profile of v4, /device:TPU:1, one launch (start us, length us, event | category | flops | bytes accessed | tf_op | source)
XLA Modules:
  0.0 98.7 jit_solution(13913496818649657924)
XLA Ops:
  0.6 1.9 %fusion.12 = (bf16[4,24,24,256]{3,2,1,0:T(8,128)(2,1)S(1)}, bf16[4,24,24,256]{3,2,1,0:T(8,128)(2,1)S(1)}) fusion(bf16[24,24,24,256]{3,2,1,0:T(8,128)(2,1)} %param.8), kind=kLoop, calls=%fused_computation.67 | loop fusion | bytes 4718592 | tf_op jit(solution)/shard_map/slice | solution.py:187
  2.6 2.1 %collective-permute-start.1 = (bf16[4,24,24,256]{3,2,1,0:T(8,128)(2,1)S(1)}, bf16[4,24,24,256]{3,2,1,0:T(8,128)(2,1)S(1)}, u32[]{:S(2)}, u32[]{:S(2)}) collective-permute-start(bf16[4,24,24,256]{3,2,1,0:T(8,128)(2,1)S(1)} %get-tuple-element.10), channel_id=1, source_target_pairs={{8,0},{16,8},{24,16},{9,1},{17,9},{25,17},{10,2},{18,10},{26,18},{... | collective-permute-start | bytes 3538952 | tf_op jit(solution)/shard_map/ppermute | solution.py:192
  4.7 4.5 %collective-permute-start = (bf16[4,24,24,256]{3,2,1,0:T(8,128)(2,1)S(1)}, bf16[4,24,24,256]{3,2,1,0:T(8,128)(2,1)S(1)}, u32[]{:S(2)}, u32[]{:S(2)}) collective-permute-start(bf16[4,24,24,256]{3,2,1,0:T(8,128)(2,1)S(1)} %get-tuple-element.11), channel_id=1, source_target_pairs={{0,8},{8,16},{16,24},{1,9},{9,17},{17,25},{2,10},{10,18},{18,26},{... | collective-permute-start | bytes 3538952 | tf_op jit(solution)/shard_map/ppermute | solution.py:192
  9.2 0.8 slice_reduce_fusion
  10.0 1.9 %fusion.11 = (bf16[24,4,24,256]{3,2,1,0:T(8,128)(2,1)S(1)}, bf16[24,4,24,256]{3,2,1,0:T(8,128)(2,1)S(1)}) fusion(bf16[24,24,24,256]{3,2,1,0:T(8,128)(2,1)} %param.8), kind=kLoop, calls=%fused_computation.66 | loop fusion | bytes 4718592 | tf_op jit(solution)/shard_map/slice | solution.py:187
  11.9 9.5 %collective-permute-done.1 = bf16[4,24,24,256]{3,2,1,0:T(8,128)(2,1)S(1)} collective-permute-done((bf16[4,24,24,256]{3,2,1,0:T(8,128)(2,1)S(1)}, bf16[4,24,24,256]{3,2,1,0:T(8,128)(2,1)S(1)}, u32[]{:S(2)}, u32[]{:S(2)}) %collective-permute-start.1) | collective-permute-done | bytes 1179680 | tf_op jit(solution)/shard_map/ppermute | solution.py:192
  21.4 0.9 collective-permute-done
  22.5 3.3 %collective-permute-start.2 = (bf16[32,4,24,256]{3,2,1,0:T(8,128)(2,1)S(1)}, bf16[32,4,24,256]{3,2,1,0:T(8,128)(2,1)S(1)}, u32[]{:S(2)}, u32[]{:S(2)}) collective-permute-start(bf16[32,4,24,256]{3,2,1,0:T(8,128)(2,1)S(1)} %pad_maximum_fusion), channel_id=1, source_target_pairs={{0,2},{2,4},{4,6},{1,3},{3,5},{5,7},{8,10},{10,12},{12,14},{9,11},... | collective-permute-start | bytes 4718600 | tf_op jit(solution)/shard_map/ppermute | solution.py:192
  26.1 1.3 %collective-permute-start.3 = (bf16[32,4,24,256]{3,2,1,0:T(8,128)(2,1)S(1)}, bf16[32,4,24,256]{3,2,1,0:T(8,128)(2,1)S(1)}, u32[]{:S(2)}, u32[]{:S(2)}) collective-permute-start(bf16[32,4,24,256]{3,2,1,0:T(8,128)(2,1)S(1)} %pad_maximum_fusion.1), channel_id=1, source_target_pairs={{2,0},{4,2},{6,4},{3,1},{5,3},{7,5},{10,8},{12,10},{14,12},{11,9},... | collective-permute-start | bytes 4718600 | tf_op jit(solution)/shard_map/ppermute | solution.py:192
  27.4 3.1 %collective-permute-start.6 = (s32[3,4]{1,0:T(4,128)S(1)}, s32[3,4]{1,0:T(4,128)S(1)}, u32[]{:S(2)}, u32[]{:S(2)}) collective-permute-start(s32[3,4]{1,0:T(4,128)S(1)} %pad_add_fusion), channel_id=1, source_target_pairs={{0,1},{2,3},{4,5},{6,7},{8,9},{10,11},{12,13},{14,15},{16,17},{18,... | collective-permute-start | bytes 152 | tf_op jit(solution)/shard_map/ppermute | solution.py:192
  30.5 1.3 %collective-permute-start.4 = (s32[3,4]{1,0:T(4,128)S(1)}, s32[3,4]{1,0:T(4,128)S(1)}, u32[]{:S(2)}, u32[]{:S(2)}) collective-permute-start(s32[3,4]{1,0:T(4,128)S(1)} %pad_add_fusion), channel_id=1, source_target_pairs={{1,0},{3,2},{5,4},{7,6},{9,8},{11,10},{13,12},{15,14},{17,16},{19,... | collective-permute-start | bytes 152 | tf_op jit(solution)/shard_map/ppermute | solution.py:192
  32.0 2.5 %pad.8 = bf16[32,32,24,256]{3,2,1,0:T(8,128)(2,1)S(1)} pad(bf16[24,24,24,256]{3,2,1,0:T(8,128)(2,1)S(1)} %bitcast.71, bf16[]{:T(256)} %constant.25.clone.1), padding=4_4x4_4x0_0x0_0 | pad | bytes 19660802 | tf_op jit(solution)/shard_map/pad | solution.py:209
  34.4 0.7 fusion.17
  35.1 0.8 select_reduce_fusion
  36.1 0.7 fusion.15
  36.8 0.7 fusion.16
  37.6 11.9 %collective-permute-done.2 = bf16[32,4,24,256]{3,2,1,0:T(8,128)(2,1)S(1)} collective-permute-done((bf16[32,4,24,256]{3,2,1,0:T(8,128)(2,1)S(1)}, bf16[32,4,24,256]{3,2,1,0:T(8,128)(2,1)S(1)}, u32[]{:S(2)}, u32[]{:S(2)}) %collective-permute-start.2) | collective-permute-done | bytes 1572896 | tf_op jit(solution)/shard_map/ppermute | solution.py:192
  49.7 4.3 %collective-permute-done.3 = bf16[32,4,24,256]{3,2,1,0:T(8,128)(2,1)S(1)} collective-permute-done((bf16[32,4,24,256]{3,2,1,0:T(8,128)(2,1)S(1)}, bf16[32,4,24,256]{3,2,1,0:T(8,128)(2,1)S(1)}, u32[]{:S(2)}, u32[]{:S(2)}) %collective-permute-start.3) | collective-permute-done | bytes 1572896 | tf_op jit(solution)/shard_map/ppermute | solution.py:192
  54.1 1.7 %fusion.10 = (bf16[32,32,4,256]{3,2,1,0:T(4,128)(2,1)S(1)}, bf16[32,32,4,256]{3,2,1,0:T(4,128)(2,1)S(1)}) fusion(bf16[32,32,24,256]{3,2,1,0:T(8,128)(2,1)S(1)} %constant_dynamic-update-slice_fusion), kind=kLoop, calls=%fused_computation.65 | loop fusion | bytes 8388608 | tf_op jit(solution)/shard_map/slice | solution.py:187
  55.8 7.8 %dynamic-slice_bitcast_fusion.2 = (bf16[1,8,8,4,256]{4,3,2,1,0:T(4,128)(2,1)S(1)}, bf16[1,8,8,4,256]{4,3,2,1,0:T(4,128)(2,1)S(1)}, bf16[1,8,8,4,256]{4,3,2,1,0:T...) fusion(bf16[32,32,4,256]{3,2,1,0:T(4,128)(2,1)S(1)} %get-tuple-, ...), kind=kLoop, calls=%fused_computation.36 | loop fusion | bytes 1572912 | tf_op jit(solution)/shard_map/stack | solution.py:226
  63.9 3.1 %collective-permute-start.5 = (bf16[3,8,8,4,256]{4,3,2,1,0:T(4,128)(2,1)S(1)}, bf16[3,8,8,4,256]{4,3,2,1,0:T(4,128)(2,1)S(1)}, u32[]{:S(2)}, u32[]{:S(2)}) collective-permute-start(bf16[3,8,8,4,256]{4,3,2,1,0:T(4,128)(2,1)S(1)} %pad_maximum_fusion.3), channel_id=1, source_target_pairs={{0,1},{2,3},{4,5},{6,7},{8,9},{10,11},{12,13},{14,15},{16,17},{18,... | collective-permute-start | bytes 1179656 | tf_op jit(solution)/shard_map/ppermute | solution.py:192
  67.1 0.7 fusion.19
  68.1 1.3 %collective-permute-start.7 = (bf16[3,8,8,4,256]{4,3,2,1,0:T(4,128)(2,1)S(1)}, bf16[3,8,8,4,256]{4,3,2,1,0:T(4,128)(2,1)S(1)}, u32[]{:S(2)}, u32[]{:S(2)}) collective-permute-start(bf16[3,8,8,4,256]{4,3,2,1,0:T(4,128)(2,1)S(1)} %pad_maximum_fusion.4), channel_id=1, source_target_pairs={{1,0},{3,2},{5,4},{7,6},{9,8},{11,10},{13,12},{15,14},{17,16},{19,... | collective-permute-start | bytes 1179656 | tf_op jit(solution)/shard_map/ppermute | solution.py:192
  69.4 5.4 %constant_dynamic-slice_fusion.3 = (bf16[8,8,24,256]{3,2,1,0:T(8,128)(2,1)S(1)}, bf16[8,8,24,256]{3,2,1,0:T(8,128)(2,1)S(1)}, bf16[8,8,24,256]{3,2,1,0:T(8,128)(2,1)S(1)}, bf16[8,8,24,256]{3,2,1,0:T(8,128)(2,1)S(1)}) fusion(bf16[32,32,24,256]{3,2,1,0:T(8,128)(2,1)S(1)} %constant_dynamic-update-slice_fusion, s32[]{:T(128)} %bitcast.10, s32[]{:T(128)} %bitcast.11, ...), kind=kLoop, calls=%fused_computation.46 | loop fusion | bytes 6291488 | tf_op jit(solution)/shard_map/dynamic_slice | solution.py:217
  74.9 1.6 %collective-permute-done.7 = bf16[3,8,8,4,256]{4,3,2,1,0:T(4,128)(2,1)S(1)} collective-permute-done((bf16[3,8,8,4,256]{4,3,2,1,0:T(4,128)(2,1)S(1)}, bf16[3,8,8,4,256]{4,3,2,1,0:T(4,128)(2,1)S(1)}, u32[]{:S(2)}, u32[]{:S(2)}) %collective-permute-start.7) | collective-permute-done | bytes 393248 | tf_op jit(solution)/shard_map/ppermute | solution.py:192
  76.7 1.0 %fusion.4 = bf16[8,8,8,256]{3,2,1,0:T(8,128)(2,1)S(1)} fusion(s32[]{:T(128)} %bitcast.38, bf16[8,8,4,256]{3,2,1,0:T(4,128)(2,1)S(1)} %get-tuple-element.23, bf16[8,8,24,256]{3,2,1,0:T(8,128)(2,1)S(1)} %get-tuple-element.3, bf16[8,8,4,256]{3,2,1,0:T(4,128)(2,1)S(1)} %get-tuple-element.26), kind=kLoop, calls=%fused_computation.23 | loop fusion | flops 786432 | bytes 1310724 | tf_op jit(solution)/shard_map/concatenate | solution.py:233
  77.7 0.9 fusion.6
  78.7 2.1 %fusion.1 = (bf16[8,8,8,256]{3,2,1,0:T(8,128)(2,1)S(1)}, bf16[8,8,8,256]{3,2,1,0:T(8,128)(2,1)S(1)}) fusion(s32[]{:T(128)} %bitcast.12, bf16[8,8,4,256]{3,2,1,0:T(4,128)(2,1)S(1)} %broadcast_in_dim.34, bf16[8,8,4,256]{3,2,1,0:T(4,128)(2,1)S(1)} %get-tuple-element.22, bf16[8,8,24,256]{3,2,1,0:T(8,128)(2,1)S(1)} %get-tuple-element.2, s32[]{:T(128)} %bitcast.26, ...), kind=kLoop, calls=%fused_computation.20 | loop fusion | flops 1572864 | bytes 2490376 | tf_op jit(solution)/shard_map/concatenate | solution.py:233
  81.5 8.4 %patches.1 = f32[4,64,320]{2,1,0:T(8,128)S(1)} custom-call(s32[4]{0:T(128)S(1)} %multiply_add_fusion.slot_ref, f32[30]{0:T(128)S(1)} %copy-done, f32[16,512]{1,0:T(8,128)S(1)} %select_maximum_fusion.dofs_ref, bf16[4,512,256]{2,1,0:T(8,128)(2,1)S(1)} %pad_maximum_fusion.2.rows_ref), custom_call_target="tpu_custom_call" | custom-call | flops 1000000000 | bytes 2097152 | tf_op jit(solution)/shard_map/patches/pallas_call | solution.py:167
  89.9 7.1 %all_to_all.5 = f32[4,64,320]{2,1,0:T(8,128)S(1)} all-to-all(f32[4,64,320]{2,1,0:T(8,128)S(1)} %patches.1), channel_id=1, replica_groups=mesh['gx'=4,'gy'=4,'gz'=2] {'gz'}, dimensions={0} | all-to-all | bytes 655360 | tf_op jit(solution)/shard_map/all_to_all | solution.py:258
  97.0 0.7 reshape.107
  97.8 0.9 copy.10
  (44 shorter events, 2.8 us)
Async XLA Ops:
  0.6 31.3 %slice-start = ((s8[7077888]{0:T(1024)(128)(4,1)}), s8[4194304]{0:T(1024)(128)(4,1)S(1)}, s32[]{:S(2)}) async-start(s8[7077888]{0:T(1024)(128)(4,1)} %bitcast.70), calls=%async_computation.1 | async-start | bytes 8388608
  2.6 18.8 %collective-permute-start.1 = (bf16[4,24,24,256]{3,2,1,0:T(8,128)(2,1)S(1)}, bf16[4,24,24,256]{3,2,1,0:T(8,128)(2,1)S(1)}, u32[]{:S(2)}, u32[]{:S(2)}) collective-permute-start(bf16[4,24,24,256]{3,2,1,0:T(8,128)(2,1)S(1)} %get-tuple-element.10), channel_id=1, source_target_pairs={{8,0},{16,8},{24,16},{9,1},{17,9},{25,17},{10,2},{18,10},{26,18},{... | collective-permute-start | bytes 3538952 | tf_op jit(solution)/shard_map/ppermute | solution.py:192
  4.7 17.6 %collective-permute-start = (bf16[4,24,24,256]{3,2,1,0:T(8,128)(2,1)S(1)}, bf16[4,24,24,256]{3,2,1,0:T(8,128)(2,1)S(1)}, u32[]{:S(2)}, u32[]{:S(2)}) collective-permute-start(bf16[4,24,24,256]{3,2,1,0:T(8,128)(2,1)S(1)} %get-tuple-element.11), channel_id=1, source_target_pairs={{0,8},{8,16},{16,24},{1,9},{9,17},{17,25},{2,10},{10,18},{18,26},{... | collective-permute-start | bytes 3538952 | tf_op jit(solution)/shard_map/ppermute | solution.py:192
  10.0 22.0 %slice-start.1 = ((s8[7077888]{0:T(1024)(128)(4,1)}), s8[2883584]{0:T(1024)(128)(4,1)S(1)}, s32[]{:S(2)}) async-start(s8[7077888]{0:T(1024)(128)(4,1)} %bitcast.70), calls=%async_computation.2 | async-start | bytes 5767168
  22.5 27.0 %collective-permute-start.2 = (bf16[32,4,24,256]{3,2,1,0:T(8,128)(2,1)S(1)}, bf16[32,4,24,256]{3,2,1,0:T(8,128)(2,1)S(1)}, u32[]{:S(2)}, u32[]{:S(2)}) collective-permute-start(bf16[32,4,24,256]{3,2,1,0:T(8,128)(2,1)S(1)} %pad_maximum_fusion), channel_id=1, source_target_pairs={{0,2},{2,4},{4,6},{1,3},{3,5},{5,7},{8,10},{10,12},{12,14},{9,11},... | collective-permute-start | bytes 4718600 | tf_op jit(solution)/shard_map/ppermute | solution.py:192
  25.8 6.0 %copy-start.3 = (bf16[4,512]{1,0:T(4,128)(2,1)S(1)}, bf16[4,512]{1,0:T(4,128)(2,1)}, u32[]{:S(2)}) copy-start(bf16[4,512]{1,0:T(4,128)(2,1)} %param.13) | copy-start | bytes 12292
  25.8 6.0 %copy-start.1 = (s32[4,512]{1,0:T(4,128)S(1)}, s32[4,512]{1,0:T(4,128)}, u32[]{:S(2)}) copy-start(s32[4,512]{1,0:T(4,128)} %param.12) | copy-start | bytes 24580
  25.8 6.0 %copy-start.4 = (bf16[256]{0:T(256)(128)(2,1)S(1)}, bf16[256]{0:T(256)(128)(2,1)}, u32[]{:S(2)}) copy-start(bf16[256]{0:T(256)(128)(2,1)} %param.9) | copy-start | bytes 1540
  26.1 27.9 %collective-permute-start.3 = (bf16[32,4,24,256]{3,2,1,0:T(8,128)(2,1)S(1)}, bf16[32,4,24,256]{3,2,1,0:T(8,128)(2,1)S(1)}, u32[]{:S(2)}, u32[]{:S(2)}) collective-permute-start(bf16[32,4,24,256]{3,2,1,0:T(8,128)(2,1)S(1)} %pad_maximum_fusion.1), channel_id=1, source_target_pairs={{2,0},{4,2},{6,4},{3,1},{5,3},{7,5},{10,8},{12,10},{14,12},{11,9},... | collective-permute-start | bytes 4718600 | tf_op jit(solution)/shard_map/ppermute | solution.py:192
  27.4 8.7 %collective-permute-start.6 = (s32[3,4]{1,0:T(4,128)S(1)}, s32[3,4]{1,0:T(4,128)S(1)}, u32[]{:S(2)}, u32[]{:S(2)}) collective-permute-start(s32[3,4]{1,0:T(4,128)S(1)} %pad_add_fusion), channel_id=1, source_target_pairs={{0,1},{2,3},{4,5},{6,7},{8,9},{10,11},{12,13},{14,15},{16,17},{18,... | collective-permute-start | bytes 152 | tf_op jit(solution)/shard_map/ppermute | solution.py:192
  30.5 6.2 %collective-permute-start.4 = (s32[3,4]{1,0:T(4,128)S(1)}, s32[3,4]{1,0:T(4,128)S(1)}, u32[]{:S(2)}, u32[]{:S(2)}) collective-permute-start(s32[3,4]{1,0:T(4,128)S(1)} %pad_add_fusion), channel_id=1, source_target_pairs={{1,0},{3,2},{5,4},{7,6},{9,8},{11,10},{13,12},{15,14},{17,16},{19,... | collective-permute-start | bytes 152 | tf_op jit(solution)/shard_map/ppermute | solution.py:192
  31.9 3.2 %copy-start.2 = (s32[4,512]{1,0:T(4,128)S(1)}, s32[4,512]{1,0:T(4,128)}, u32[]{:S(2)}) copy-start(s32[4,512]{1,0:T(4,128)} %param.10) | copy-start | bytes 24580
  31.9 4.0 %copy-start.5 = (s32[4]{0:T(128)S(1)}, s32[4]{0:T(128)}, u32[]{:S(2)}) copy-start(s32[4]{0:T(128)} %param.14) | copy-start | bytes 52
  63.9 10.9 %collective-permute-start.5 = (bf16[3,8,8,4,256]{4,3,2,1,0:T(4,128)(2,1)S(1)}, bf16[3,8,8,4,256]{4,3,2,1,0:T(4,128)(2,1)S(1)}, u32[]{:S(2)}, u32[]{:S(2)}) collective-permute-start(bf16[3,8,8,4,256]{4,3,2,1,0:T(4,128)(2,1)S(1)} %pad_maximum_fusion.3), channel_id=1, source_target_pairs={{0,1},{2,3},{4,5},{6,7},{8,9},{10,11},{12,13},{14,15},{16,17},{18,... | collective-permute-start | bytes 1179656 | tf_op jit(solution)/shard_map/ppermute | solution.py:192
  68.1 8.5 %collective-permute-start.7 = (bf16[3,8,8,4,256]{4,3,2,1,0:T(4,128)(2,1)S(1)}, bf16[3,8,8,4,256]{4,3,2,1,0:T(4,128)(2,1)S(1)}, u32[]{:S(2)}, u32[]{:S(2)}) collective-permute-start(bf16[3,8,8,4,256]{4,3,2,1,0:T(4,128)(2,1)S(1)} %pad_maximum_fusion.4), channel_id=1, source_target_pairs={{1,0},{3,2},{5,4},{7,6},{9,8},{11,10},{13,12},{15,14},{17,16},{19,... | collective-permute-start | bytes 1179656 | tf_op jit(solution)/shard_map/ppermute | solution.py:192
  80.8 0.7 copy-start

commit v5 on v4

--- a/solution.py
+++ b/solution.py
@@ -221,9 +221,8 @@
     count = localization.shape[0]
     rising = [p for p in range(count) if p != 1]
     falling = [p for p in range(count) if p != 0]
-    z_last, z_first = edges(wide, 2)
-    sent_up = jnp.stack([window(z_last, upper, p) for p in rising])
-    sent_down = jnp.stack([window(z_first, lower, p) for p in falling])
+    sent_up = jnp.stack([edges(window(wide, upper, p), 2)[0] for p in rising])
+    sent_down = jnp.stack([edges(window(wide, lower, p), 2)[1] for p in falling])
     z_before, z_after = exchanged(sent_up, sent_down, "gz")
     nothing = jnp.zeros((BOX, BOX, HW, fine_rhs.shape[-1]), fine_rhs.dtype)
     rows = []

time: 99.8 us -> 107 us (1.072)
  local copies, waits for them, and re-layouts: 27.6 us -> 40.9 us
  waiting for transfers between devices: 28.2 us -> 18.2 us
  other arithmetic: 6.2 us -> 8.61 us
    ppermute x8, waiting for transfers between devices: 28.2 us -> 18.2 us  [exchanged(): return (lax.ppermute(last, axis, up), lax.ppermute(first, axis, down))]
    dynamic_update_slice x4, local copies, waits for them, and re-layouts: 0.39 us -> 7.58 us  [boxes(): wide = lax.dynamic_update_slice(wide, piece, at + (0, 0))]
    pad x1, local copies, waits for them, and re-layouts: 2.46 us -> 6.51 us  [boxes(): lax.pad(fine_rhs, jnp.zeros((), fine_rhs.dtype), [side, side, none, none])]
    another operation x1, local copies, waits for them, and re-layouts: 7.81 us -> 9.69 us  [boxes(): jnp.stack([edges(window(wide, lower, p), 2)[1] for p in falling])]
    dynamic_slice x1, local copies, waits for them, and re-layouts: 5.41 us -> 7.2 us  [window(): lax.dynamic_slice(source, (at[0, p], at[1, p], zero, zero), (BOX, BOX) +...]
    slice x5 -> x4, local copies, waits for them, and re-layouts: 5.59 us -> 3.92 us  [edges(): lax.slice_in_dim(array, 0, HW, axis=dim)]
    concatenate x1, other arithmetic: 0.19 us -> 1.36 us  [boxes(): jnp.concatenate([edges(before, 1)[0], y_last, edges(after, 1)[0]], axis=0)]
    concatenate x1, other arithmetic: 0.19 us -> 1.36 us  [boxes(): jnp.concatenate([edges(before, 1)[1], y_first, edges(after, 1)[1]], axis=0)]
  transfers between devices with their start and end apart: 8 -> 8, of which waited for: 5 -> 4; matrix products, arithmetic and copies ran while one was open for 15% -> 25% of each run, Pallas kernels for 0% -> 0%
where the time goes in v5:
time: 107 us; the launch traced here: 106 us
  local copies, waits for them, and re-layouts  40.9 us (38%)
  starting transfers between devices  20.9 us (20%)
  waiting for transfers between devices  18.2 us (17%)
  other arithmetic  8.61 us (8%)
  Pallas kernels  8.43 us (8%)
  blocking collectives  7.89 us (7%)
    ppermute x8, starting transfers between devices, exchanged(): return (lax.ppermute(last, axis, up), lax.ppermute(first, axis, down))  20.9 us
    ppermute x8, waiting for transfers between devices, exchanged(): return (lax.ppermute(last, axis, up), lax.ppermute(first, axis, down))  18.2 us
    another operation x1, local copies, waits for them, and re-layouts, boxes(): jnp.stack([edges(window(wide, lower, p), 2)[1] for p in falling])  9.69 us
    pallas_call x1, Pallas kernels, coarse_parts(): pl.pallas_call(patch_kernel, out_shape=jax.ShapeDtypeStruct((slot_count,...  8.43 us
    all_to_all x1, blocking collectives, local(): lax.all_to_all(results, 'gz', split_axis=0, concat_axis=0, tiled=True)  7.89 us
    dynamic_update_slice x4, local copies, waits for them, and re-layouts, boxes(): wide = lax.dynamic_update_slice(wide, piece, at + (0, 0))  7.58 us
    dynamic_slice x1, local copies, waits for them, and re-layouts, window(): lax.dynamic_slice(source, (at[0, p], at[1, p], zero, zero), (BOX, BOX) +...  7.2 us
    pad x1, local copies, waits for them, and re-layouts, boxes(): lax.pad(fine_rhs, jnp.zeros((), fine_rhs.dtype), [side, side, none, none])  6.51 us
  transfers between devices with their start and end apart: 8, of which 4 were waited for; matrix products, arithmetic and copies ran while one was open for 25% of the time, Pallas kernels for 0%

profile of v5, /device:TPU:1, one launch (start us, length us, event | category | flops | bytes accessed | tf_op | source)
XLA Modules:
  0.0 105.9 jit_solution(9998620136834700189)
XLA Ops:
  0.6 1.9 %fusion.11 = (bf16[4,24,24,256]{3,2,1,0:T(8,128)(2,1)S(1)}, bf16[4,24,24,256]{3,2,1,0:T(8,128)(2,1)S(1)}) fusion(bf16[24,24,24,256]{3,2,1,0:T(8,128)(2,1)} %param.8), kind=kLoop, calls=%fused_computation.66 | loop fusion | bytes 4718592 | tf_op jit(solution)/shard_map/slice | solution.py:187
  2.6 2.1 %collective-permute-start.1 = (bf16[4,24,24,256]{3,2,1,0:T(8,128)(2,1)S(1)}, bf16[4,24,24,256]{3,2,1,0:T(8,128)(2,1)S(1)}, u32[]{:S(2)}, u32[]{:S(2)}) collective-permute-start(bf16[4,24,24,256]{3,2,1,0:T(8,128)(2,1)S(1)} %get-tuple-element.14), channel_id=1, source_target_pairs={{8,0},{16,8},{24,16},{9,1},{17,9},{25,17},{10,2},{18,10},{26,18},{... | collective-permute-start | bytes 3538952 | tf_op jit(solution)/shard_map/ppermute | solution.py:192
  4.7 4.5 %collective-permute-start = (bf16[4,24,24,256]{3,2,1,0:T(8,128)(2,1)S(1)}, bf16[4,24,24,256]{3,2,1,0:T(8,128)(2,1)S(1)}, u32[]{:S(2)}, u32[]{:S(2)}) collective-permute-start(bf16[4,24,24,256]{3,2,1,0:T(8,128)(2,1)S(1)} %get-tuple-element.15), channel_id=1, source_target_pairs={{0,8},{8,16},{16,24},{1,9},{9,17},{17,25},{2,10},{10,18},{18,26},{... | collective-permute-start | bytes 3538952 | tf_op jit(solution)/shard_map/ppermute | solution.py:192
  9.2 0.8 slice_reduce_fusion
  10.0 1.9 %fusion.10 = (bf16[24,4,24,256]{3,2,1,0:T(8,128)(2,1)S(1)}, bf16[24,4,24,256]{3,2,1,0:T(8,128)(2,1)S(1)}) fusion(bf16[24,24,24,256]{3,2,1,0:T(8,128)(2,1)} %param.8), kind=kLoop, calls=%fused_computation.65 | loop fusion | bytes 4718592 | tf_op jit(solution)/shard_map/slice | solution.py:187
  11.9 9.2 %collective-permute-done.1 = bf16[4,24,24,256]{3,2,1,0:T(8,128)(2,1)S(1)} collective-permute-done((bf16[4,24,24,256]{3,2,1,0:T(8,128)(2,1)S(1)}, bf16[4,24,24,256]{3,2,1,0:T(8,128)(2,1)S(1)}, u32[]{:S(2)}, u32[]{:S(2)}) %collective-permute-start.1) | collective-permute-done | bytes 1179680 | tf_op jit(solution)/shard_map/ppermute | solution.py:192
  21.1 1.2 %collective-permute-done = bf16[4,24,24,256]{3,2,1,0:T(8,128)(2,1)S(1)} collective-permute-done((bf16[4,24,24,256]{3,2,1,0:T(8,128)(2,1)S(1)}, bf16[4,24,24,256]{3,2,1,0:T(8,128)(2,1)S(1)}, u32[]{:S(2)}, u32[]{:S(2)}) %collective-permute-start) | collective-permute-done | bytes 1179680 | tf_op jit(solution)/shard_map/ppermute | solution.py:192
  22.3 1.4 %pad_maximum_fusion = bf16[32,4,24,256]{3,2,1,0:T(8,128)(2,1)} fusion(bf16[4,4,24,256]{3,2,1,0:T(8,128)(2,1)S(1)} %get-tuple-element.19, bf16[24,4,24,256]{3,2,1,0:T(8,128)(2,1)S(1)} %get-tuple-element.13, bf16[4,4,24,256]{3,2,1,0:T(8,128)(2,1)S(1)} %get-tuple-element.17), kind=kLoop, calls=%fused_computation.2 | loop fusion | flops 1572864 | bytes 3145728 | tf_op jit(solution)/shard_map/concatenate | solution.py:205
  23.7 4.4 %collective-permute-start.2 = (bf16[32,4,24,256]{3,2,1,0:T(8,128)(2,1)}, bf16[32,4,24,256]{3,2,1,0:T(8,128)(2,1)}, u32[]{:S(2)}, u32[]{:S(2)}) collective-permute-start(bf16[32,4,24,256]{3,2,1,0:T(8,128)(2,1)} %pad_maximum_fusion), channel_id=1, source_target_pairs={{0,2},{2,4},{4,6},{1,3},{3,5},{5,7},{8,10},{10,12},{12,14},{9,11},... | collective-permute-start | bytes 4718600 | tf_op jit(solution)/shard_map/ppermute | solution.py:192
  28.0 1.4 %pad_maximum_fusion.1 = bf16[32,4,24,256]{3,2,1,0:T(8,128)(2,1)} fusion(bf16[4,4,24,256]{3,2,1,0:T(8,128)(2,1)S(1)} %get-tuple-element.18, bf16[24,4,24,256]{3,2,1,0:T(8,128)(2,1)S(1)} %get-tuple-element.12, bf16[4,4,24,256]{3,2,1,0:T(8,128)(2,1)S(1)} %get-tuple-element.16), kind=kLoop, calls=%fused_computation.3 | loop fusion | flops 1572864 | bytes 3145728 | tf_op jit(solution)/shard_map/concatenate | solution.py:206
  29.4 1.3 %collective-permute-start.3 = (bf16[32,4,24,256]{3,2,1,0:T(8,128)(2,1)}, bf16[32,4,24,256]{3,2,1,0:T(8,128)(2,1)}, u32[]{:S(2)}, u32[]{:S(2)}) collective-permute-start(bf16[32,4,24,256]{3,2,1,0:T(8,128)(2,1)} %pad_maximum_fusion.1), channel_id=1, source_target_pairs={{2,0},{4,2},{6,4},{3,1},{5,3},{7,5},{10,8},{12,10},{14,12},{11,9},... | collective-permute-start | bytes 4718600 | tf_op jit(solution)/shard_map/ppermute | solution.py:192
  30.7 3.1 %collective-permute-start.6 = (s32[3,4]{1,0:T(4,128)S(1)}, s32[3,4]{1,0:T(4,128)S(1)}, u32[]{:S(2)}, u32[]{:S(2)}) collective-permute-start(s32[3,4]{1,0:T(4,128)S(1)} %pad_add_fusion), channel_id=1, source_target_pairs={{0,1},{2,3},{4,5},{6,7},{8,9},{10,11},{12,13},{14,15},{16,17},{18,... | collective-permute-start | bytes 152 | tf_op jit(solution)/shard_map/ppermute | solution.py:192
  33.9 1.3 %collective-permute-start.4 = (s32[3,4]{1,0:T(4,128)S(1)}, s32[3,4]{1,0:T(4,128)S(1)}, u32[]{:S(2)}, u32[]{:S(2)}) collective-permute-start(s32[3,4]{1,0:T(4,128)S(1)} %pad_add_fusion), channel_id=1, source_target_pairs={{1,0},{3,2},{5,4},{7,6},{9,8},{11,10},{13,12},{15,14},{17,16},{19,... | collective-permute-start | bytes 152 | tf_op jit(solution)/shard_map/ppermute | solution.py:192
  35.3 6.5 %pad.8 = bf16[32,32,24,256]{3,2,1,0:T(8,128)(2,1)} pad(bf16[24,24,24,256]{3,2,1,0:T(8,128)(2,1)S(1)} %bitcast.71, bf16[]{:T(256)} %constant.25.clone.1), padding=4_4x4_4x0_0x0_0 | pad | bytes 19660802 | tf_op jit(solution)/shard_map/pad | solution.py:209
  42.5 0.8 select_reduce_fusion
  44.8 1.1 %constant_dynamic-update-slice_fusion.3 = bf16[32,32,24,256]{3,2,1,0:T(8,128)(2,1)} fusion(bf16[32,32,24,256]{3,2,1,0:T(8,128)(2,1)} %pad.8, bf16[4,24,24,256]{3,2,1,0:T(8,128)(2,1)S(1)} %collective-permute-done), kind=kLoop, calls=%fused_computation.50 | loop fusion | bytes 2359296 | tf_op jit(solution)/shard_map/dynamic_update_slice | solution.py:212
  45.9 1.1 %constant_dynamic-update-slice_fusion.2 = bf16[32,32,24,256]{3,2,1,0:T(8,128)(2,1)} fusion(bf16[32,32,24,256]{3,2,1,0:T(8,128)(2,1)} %constant_dynamic-update-slice_fusion.3, bf16[4,24,24,256]{3,2,1,0:T(8,128)(2,1)S(1)} %collective-permute-done.1), kind=kLoop, calls=%fused_computation.49 | loop fusion | bytes 2359296 | tf_op jit(solution)/shard_map/dynamic_update_slice | solution.py:212
  47.1 3.9 %collective-permute-done.2 = bf16[32,4,24,256]{3,2,1,0:T(8,128)(2,1)} collective-permute-done((bf16[32,4,24,256]{3,2,1,0:T(8,128)(2,1)}, bf16[32,4,24,256]{3,2,1,0:T(8,128)(2,1)}, u32[]{:S(2)}, u32[]{:S(2)}) %collective-permute-start.2) | collective-permute-done | bytes 1572896 | tf_op jit(solution)/shard_map/ppermute | solution.py:192
  51.0 2.7 %constant_dynamic-update-slice_fusion.1 = bf16[32,32,24,256]{3,2,1,0:T(8,128)(2,1)} fusion(bf16[32,32,24,256]{3,2,1,0:T(8,128)(2,1)} %constant_dynamic-update-slice_fusion.2, bf16[32,4,24,256]{3,2,1,0:T(8,128)(2,1)} %collective-permute-done.2), kind=kLoop, calls=%fused_computation.48 | loop fusion | bytes 3145728 | tf_op jit(solution)/shard_map/dynamic_update_slice | solution.py:212
  53.7 3.9 %collective-permute-done.3 = bf16[32,4,24,256]{3,2,1,0:T(8,128)(2,1)} collective-permute-done((bf16[32,4,24,256]{3,2,1,0:T(8,128)(2,1)}, bf16[32,4,24,256]{3,2,1,0:T(8,128)(2,1)}, u32[]{:S(2)}, u32[]{:S(2)}) %collective-permute-start.3) | collective-permute-done | bytes 1572896 | tf_op jit(solution)/shard_map/ppermute | solution.py:192
  57.6 2.7 %constant_dynamic-update-slice_fusion = bf16[32,32,24,256]{3,2,1,0:T(8,128)(2,1)} fusion(bf16[32,32,24,256]{3,2,1,0:T(8,128)(2,1)} %constant_dynamic-update-slice_fusion.1, bf16[32,4,24,256]{3,2,1,0:T(8,128)(2,1)} %collective-permute-done.3), kind=kLoop, calls=%fused_computation.47 | loop fusion | bytes 3145728 | tf_op jit(solution)/shard_map/dynamic_update_slice | solution.py:212
  60.3 9.7 %dynamic-slice_bitcast_fusion.2 = (bf16[1,8,8,4,256]{4,3,2,1,0:T(4,128)(2,1)S(1)}, bf16[1,8,8,4,256]{4,3,2,1,0:T(4,128)(2,1)S(1)}, bf16[1,8,8,4,256]{4,3,2,1,0:T...) fusion(bf16[32,32,24,256]{3,2,1,0:T(8,128)(2,1)} %constant_dyna, ...), kind=kLoop, calls=%fused_computation.35 | loop fusion | bytes 1572916 | tf_op jit(solution)/shard_map/stack | solution.py:225
  70.3 3.0 %collective-permute-start.5 = (bf16[3,8,8,4,256]{4,3,2,1,0:T(4,128)(2,1)S(1)}, bf16[3,8,8,4,256]{4,3,2,1,0:T(4,128)(2,1)S(1)}, u32[]{:S(2)}, u32[]{:S(2)}) collective-permute-start(bf16[3,8,8,4,256]{4,3,2,1,0:T(4,128)(2,1)S(1)} %pad_maximum_fusion.3), channel_id=1, source_target_pairs={{0,1},{2,3},{4,5},{6,7},{8,9},{10,11},{12,13},{14,15},{16,17},{18,... | collective-permute-start | bytes 1179656 | tf_op jit(solution)/shard_map/ppermute | solution.py:192
  74.2 1.3 %collective-permute-start.7 = (bf16[3,8,8,4,256]{4,3,2,1,0:T(4,128)(2,1)S(1)}, bf16[3,8,8,4,256]{4,3,2,1,0:T(4,128)(2,1)S(1)}, u32[]{:S(2)}, u32[]{:S(2)}) collective-permute-start(bf16[3,8,8,4,256]{4,3,2,1,0:T(4,128)(2,1)S(1)} %pad_maximum_fusion.4), channel_id=1, source_target_pairs={{1,0},{3,2},{5,4},{7,6},{9,8},{11,10},{13,12},{15,14},{17,16},{19,... | collective-permute-start | bytes 1179656 | tf_op jit(solution)/shard_map/ppermute | solution.py:192
  75.5 7.2 %constant_dynamic-slice_fusion.3 = (bf16[8,8,24,256]{3,2,1,0:T(8,128)(2,1)S(1)}, bf16[8,8,24,256]{3,2,1,0:T(8,128)(2,1)S(1)}, bf16[8,8,24,256]{3,2,1,0:T(8,128)(2,1)S(1)}, bf16[8,8,24,256]{3,2,1,0:T(8,128)(2,1)S(1)}) fusion(bf16[32,32,24,256]{3,2,1,0:T(8,128)(2,1)} %constant_dynamic-update-slice_fusion, s32[]{:T(128)} %bitcast.10, s32[]{:T(128)} %bitcast.11, ...), kind=kLoop, calls=%fused_computation.46 | loop fusion | bytes 6291488 | tf_op jit(solution)/shard_map/dynamic_slice | solution.py:217
  83.1 1.0 fusion.4
  84.1 1.0 fusion.6
  85.2 2.0 %fusion.1 = (bf16[8,8,8,256]{3,2,1,0:T(8,128)(2,1)S(1)}, bf16[8,8,8,256]{3,2,1,0:T(8,128)(2,1)S(1)}) fusion(s32[]{:T(128)} %bitcast.12, bf16[8,8,4,256]{3,2,1,0:T(4,128)(2,1)S(1)} %broadcast_in_dim.34, bf16[8,8,4,256]{3,2,1,0:T(4,128)(2,1)S(1)} %get-tuple-element.20, bf16[8,8,24,256]{3,2,1,0:T(8,128)(2,1)S(1)} %get-tuple-element.2, s32[]{:T(128)} %bitcast.26, ...), kind=kLoop, calls=%fused_computation.20 | loop fusion | flops 1572864 | bytes 2490376 | tf_op jit(solution)/shard_map/concatenate | solution.py:232
  87.9 8.4 %patches.1 = f32[4,64,320]{2,1,0:T(8,128)S(1)} custom-call(s32[4]{0:T(128)S(1)} %multiply_add_fusion.slot_ref, f32[30]{0:T(128)S(1)} %copy-done, f32[16,512]{1,0:T(8,128)S(1)} %select_maximum_fusion.dofs_ref, bf16[4,512,256]{2,1,0:T(8,128)(2,1)S(1)} %pad_maximum_fusion.2.rows_ref), custom_call_target="tpu_custom_call" | custom-call | flops 1000000000 | bytes 2097152 | tf_op jit(solution)/shard_map/patches/pallas_call | solution.py:167
  96.3 7.9 %all_to_all.5 = f32[4,64,320]{2,1,0:T(8,128)S(1)} all-to-all(f32[4,64,320]{2,1,0:T(8,128)S(1)} %patches.1), channel_id=1, replica_groups=mesh['gx'=4,'gy'=4,'gz'=2] {'gz'}, dimensions={0} | all-to-all | bytes 655360 | tf_op jit(solution)/shard_map/all_to_all | solution.py:257
  104.2 0.7 reshape.107
  105.0 0.9 copy.10
  (43 shorter events, 4.6 us)
Async XLA Ops:
  0.6 34.6 %slice-start = ((s8[7077888]{0:T(1024)(128)(4,1)}), s8[4194304]{0:T(1024)(128)(4,1)S(1)}, s32[]{:S(2)}) async-start(s8[7077888]{0:T(1024)(128)(4,1)} %bitcast.70), calls=%async_computation.1 | async-start | bytes 8388608
  2.6 18.5 %collective-permute-start.1 = (bf16[4,24,24,256]{3,2,1,0:T(8,128)(2,1)S(1)}, bf16[4,24,24,256]{3,2,1,0:T(8,128)(2,1)S(1)}, u32[]{:S(2)}, u32[]{:S(2)}) collective-permute-start(bf16[4,24,24,256]{3,2,1,0:T(8,128)(2,1)S(1)} %get-tuple-element.14), channel_id=1, source_target_pairs={{8,0},{16,8},{24,16},{9,1},{17,9},{25,17},{10,2},{18,10},{26,18},{... | collective-permute-start | bytes 3538952 | tf_op jit(solution)/shard_map/ppermute | solution.py:192
  4.7 17.6 %collective-permute-start = (bf16[4,24,24,256]{3,2,1,0:T(8,128)(2,1)S(1)}, bf16[4,24,24,256]{3,2,1,0:T(8,128)(2,1)S(1)}, u32[]{:S(2)}, u32[]{:S(2)}) collective-permute-start(bf16[4,24,24,256]{3,2,1,0:T(8,128)(2,1)S(1)} %get-tuple-element.15), channel_id=1, source_target_pairs={{0,8},{8,16},{16,24},{1,9},{9,17},{17,25},{2,10},{10,18},{18,26},{... | collective-permute-start | bytes 3538952 | tf_op jit(solution)/shard_map/ppermute | solution.py:192
  10.0 25.3 %slice-start.1 = ((s8[7077888]{0:T(1024)(128)(4,1)}), s8[2883584]{0:T(1024)(128)(4,1)S(1)}, s32[]{:S(2)}) async-start(s8[7077888]{0:T(1024)(128)(4,1)} %bitcast.70), calls=%async_computation.2 | async-start | bytes 5767168
  23.7 27.3 %collective-permute-start.2 = (bf16[32,4,24,256]{3,2,1,0:T(8,128)(2,1)}, bf16[32,4,24,256]{3,2,1,0:T(8,128)(2,1)}, u32[]{:S(2)}, u32[]{:S(2)}) collective-permute-start(bf16[32,4,24,256]{3,2,1,0:T(8,128)(2,1)} %pad_maximum_fusion), channel_id=1, source_target_pairs={{0,2},{2,4},{4,6},{1,3},{3,5},{5,7},{8,10},{10,12},{12,14},{9,11},... | collective-permute-start | bytes 4718600 | tf_op jit(solution)/shard_map/ppermute | solution.py:192
  28.0 7.1 %copy-start.3 = (bf16[4,512]{1,0:T(4,128)(2,1)S(1)}, bf16[4,512]{1,0:T(4,128)(2,1)}, u32[]{:S(2)}) copy-start(bf16[4,512]{1,0:T(4,128)(2,1)} %param.13) | copy-start | bytes 12292
  28.0 7.2 %copy-start.1 = (s32[4,512]{1,0:T(4,128)S(1)}, s32[4,512]{1,0:T(4,128)}, u32[]{:S(2)}) copy-start(s32[4,512]{1,0:T(4,128)} %param.12) | copy-start | bytes 24580
  28.0 7.2 %copy-start.4 = (bf16[256]{0:T(256)(128)(2,1)S(1)}, bf16[256]{0:T(256)(128)(2,1)}, u32[]{:S(2)}) copy-start(bf16[256]{0:T(256)(128)(2,1)} %param.9) | copy-start | bytes 1540
  29.4 28.2 %collective-permute-start.3 = (bf16[32,4,24,256]{3,2,1,0:T(8,128)(2,1)}, bf16[32,4,24,256]{3,2,1,0:T(8,128)(2,1)}, u32[]{:S(2)}, u32[]{:S(2)}) collective-permute-start(bf16[32,4,24,256]{3,2,1,0:T(8,128)(2,1)} %pad_maximum_fusion.1), channel_id=1, source_target_pairs={{2,0},{4,2},{6,4},{3,1},{5,3},{7,5},{10,8},{12,10},{14,12},{11,9},... | collective-permute-start | bytes 4718600 | tf_op jit(solution)/shard_map/ppermute | solution.py:192
  30.7 12.8 %collective-permute-start.6 = (s32[3,4]{1,0:T(4,128)S(1)}, s32[3,4]{1,0:T(4,128)S(1)}, u32[]{:S(2)}, u32[]{:S(2)}) collective-permute-start(s32[3,4]{1,0:T(4,128)S(1)} %pad_add_fusion), channel_id=1, source_target_pairs={{0,1},{2,3},{4,5},{6,7},{8,9},{10,11},{12,13},{14,15},{16,17},{18,... | collective-permute-start | bytes 152 | tf_op jit(solution)/shard_map/ppermute | solution.py:192
  33.9 10.3 %collective-permute-start.4 = (s32[3,4]{1,0:T(4,128)S(1)}, s32[3,4]{1,0:T(4,128)S(1)}, u32[]{:S(2)}, u32[]{:S(2)}) collective-permute-start(s32[3,4]{1,0:T(4,128)S(1)} %pad_add_fusion), channel_id=1, source_target_pairs={{1,0},{3,2},{5,4},{7,6},{9,8},{11,10},{13,12},{15,14},{17,16},{19,... | collective-permute-start | bytes 152 | tf_op jit(solution)/shard_map/ppermute | solution.py:192
  35.3 7.2 %copy-start.2 = (s32[4,512]{1,0:T(4,128)S(1)}, s32[4,512]{1,0:T(4,128)}, u32[]{:S(2)}) copy-start(s32[4,512]{1,0:T(4,128)} %param.10) | copy-start | bytes 24580
  35.3 8.0 %copy-start.5 = (s32[4]{0:T(128)S(1)}, s32[4]{0:T(128)}, u32[]{:S(2)}) copy-start(s32[4]{0:T(128)} %param.14) | copy-start | bytes 52
  70.3 12.5 %collective-permute-start.5 = (bf16[3,8,8,4,256]{4,3,2,1,0:T(4,128)(2,1)S(1)}, bf16[3,8,8,4,256]{4,3,2,1,0:T(4,128)(2,1)S(1)}, u32[]{:S(2)}, u32[]{:S(2)}) collective-permute-start(bf16[3,8,8,4,256]{4,3,2,1,0:T(4,128)(2,1)S(1)} %pad_maximum_fusion.3), channel_id=1, source_target_pairs={{0,1},{2,3},{4,5},{6,7},{8,9},{10,11},{12,13},{14,15},{16,17},{18,... | collective-permute-start | bytes 1179656 | tf_op jit(solution)/shard_map/ppermute | solution.py:192
  74.2 8.7 %collective-permute-start.7 = (bf16[3,8,8,4,256]{4,3,2,1,0:T(4,128)(2,1)S(1)}, bf16[3,8,8,4,256]{4,3,2,1,0:T(4,128)(2,1)S(1)}, u32[]{:S(2)}, u32[]{:S(2)}) collective-permute-start(bf16[3,8,8,4,256]{4,3,2,1,0:T(4,128)(2,1)S(1)} %pad_maximum_fusion.4), channel_id=1, source_target_pairs={{1,0},{3,2},{5,4},{7,6},{9,8},{11,10},{13,12},{15,14},{17,16},{19,... | collective-permute-start | bytes 1179656 | tf_op jit(solution)/shard_map/ppermute | solution.py:192
  87.2 0.7 copy-start
